TPU v7x, 32 devices: a whole 2x2x4 slice. The times are simulated.
32 devices in a mesh: dp: 2 (over y), expert: 16 (over z, x, core).
Axes of the slice: x: 2, y: 2, z: 4, core: 2. Of those that a mesh axis runs over, the one named last changes fastest.
Arguments:
- tokens: bfloat16 [4096, 2048], P(('dp', 'expert')), may hold values from -6 to 6
- out_grad: bfloat16 [4096, 2048], P(('dp', 'expert')), may hold values from -6 to 6
- routes: int32 [4096, 6], P(('dp', 'expert')), may hold values from 0 to 15, all different within a row; in each aligned block of 128 rows (0 to 127, 128 to 255, ...) at most 49 rows name the same one
- gate_weights: bfloat16 [4096, 6], P(('dp', 'expert')), may hold values from 0.049804688 to 0.59765625
- saved_preacts: bfloat16 [2, 16, 784, 1408], P('dp', 'expert'), may hold values from -6 to 6
- gate_up: bfloat16 [16, 2048, 1408], P('expert', 'dp'), may hold values from -0.125 to 0.125
- down_proj: bfloat16 [16, 704, 2048], P('expert', 'dp'), may hold values from -0.21875 to 0.21875
Outputs:
- grad_tokens: bfloat16 [4096, 2048], P(('dp', 'expert'))
- grad_gates: bfloat16 [4096, 6], P(('dp', 'expert'))
- grad_gate_up: float32 [16, 2048, 1408], P('expert', 'dp')
- grad_down: float32 [16, 704, 2048], P('expert', 'dp')
Inputs may be any that keep to these rules, and one draw needn't show every extreme that they name: `routes`: each token names 6 different experts. Within the 128 rows of one device no expert is named by more than 49 rows, a bound that some block reaches.
All inputs are finite; a program needn't handle non-finite values.
Results may differ from a plain program's by a relative error of at most 0.0095.
Values may be sent and summed in bfloat16 or wider, within the bound.
No kernel may reach another device: no remote copies, remote signals or barrier semaphores. Data moves between devices by JAX's collectives and lax.ppermute only.
A program may use at most 128 MiB of HBM per device.

v0:
```python
import jax
import jax.numpy as jnp
from jax import lax
from jax.sharding import PartitionSpec as P


def find_slots(routes, experts, capacity):
    flat = routes.reshape(-1)
    onehot = (flat[:, None] == jnp.arange(experts, dtype=jnp.int32)[None, :]).astype(jnp.int32)
    before = jnp.cumsum(onehot, axis=0) - onehot
    position = jnp.sum(before * onehot, axis=1)
    return flat * capacity + position


def on_device(tokens, out_grad, routes, gate_weights, saved_preacts, gate_up, down_proj):
    experts = lax.axis_size("expert")
    groups = lax.axis_size("dp")
    tok_rows, top = routes.shape
    width = tokens.shape[1]
    slot_total = saved_preacts.shape[2]
    capacity = slot_total // experts
    hidden = saved_preacts.shape[3] // 2
    slot_index = find_slots(routes, experts, capacity)
    owner_row = jnp.arange(tok_rows * top, dtype=jnp.int32) // top
    send_x = jnp.zeros((slot_total, width), jnp.bfloat16).at[slot_index].set(tokens[owner_row])
    send_dy = jnp.zeros((slot_total, width), jnp.bfloat16).at[slot_index].set(out_grad[owner_row])
    send_g = jnp.zeros((slot_total,), jnp.bfloat16).at[slot_index].set(gate_weights.reshape(-1))
    recv_x, recv_dy, recv_g = (
        lax.all_to_all(
            send_x.reshape(experts, capacity, width),
            "expert",
            split_axis=0,
            concat_axis=0,
            tiled=True,
        ),
        lax.all_to_all(
            send_dy.reshape(experts, capacity, width),
            "expert",
            split_axis=0,
            concat_axis=0,
            tiled=True,
        ),
        lax.all_to_all(
            send_g.reshape(experts, capacity), "expert", split_axis=0, concat_axis=0, tiled=True
        ),
    )
    x_rows = recv_x.reshape(slot_total, width)
    dy_rows = recv_dy.reshape(slot_total, width)
    g_rows = recv_g.reshape(slot_total).astype(jnp.float32)[:, None]
    saved_rows = saved_preacts[0, 0]
    gate_pre = saved_rows[:, :hidden].astype(jnp.float32)
    up_pre = saved_rows[:, hidden:].astype(jnp.float32)
    sigmoid_gate = jax.nn.sigmoid(gate_pre)
    act = (gate_pre * sigmoid_gate * up_pre).astype(jnp.bfloat16)
    act_grad = lax.dot_general(
        dy_rows,
        lax.all_gather(down_proj[0], "dp", axis=0, tiled=True),
        (((1,), (1,)), ((), ())),
        preferred_element_type=jnp.float32,
    )
    gate_grad_rows = (
        jnp.sum(act.astype(jnp.float32) * act_grad, axis=1) / jnp.sqrt(jnp.float32(width))
    ).astype(jnp.bfloat16)
    scaled_grad = g_rows * act_grad
    grad_gate = scaled_grad * up_pre * sigmoid_gate * (1.0 + gate_pre * (1.0 - sigmoid_gate))
    grad_up = scaled_grad * gate_pre * sigmoid_gate
    pre_grad = jnp.concatenate([grad_gate, grad_up], axis=1).astype(jnp.bfloat16)
    scaled_dy = (g_rows * dy_rows.astype(jnp.float32)).astype(jnp.bfloat16)
    row_grad = lax.dot_general(
        pre_grad,
        lax.all_gather(gate_up[0], "dp", axis=0, tiled=True),
        (((1,), (1,)), ((), ())),
        preferred_element_type=jnp.float32,
    ).astype(jnp.bfloat16)
    back_rows, back_gate = (
        lax.all_to_all(
            row_grad.reshape(experts, capacity, width),
            "expert",
            split_axis=0,
            concat_axis=0,
            tiled=True,
        ),
        lax.all_to_all(
            gate_grad_rows.reshape(experts, capacity),
            "expert",
            split_axis=0,
            concat_axis=0,
            tiled=True,
        ),
    )
    picked = (
        back_rows.reshape(slot_total, width)[slot_index]
        .astype(jnp.float32)
        .reshape(tok_rows, top, width)
    )
    grad_tokens = jnp.sum(picked, axis=1).astype(jnp.bfloat16)
    grad_gates = back_gate.reshape(slot_total)[slot_index].reshape(tok_rows, top)
    grad_scale = 1.0 / jnp.sqrt(jnp.float32(groups * tok_rows * top))
    columns = x_rows
    grad_gu = lax.psum_scatter(
        lax.dot_general(
            columns, pre_grad, (((0,), (0,)), ((), ())), preferred_element_type=jnp.float32
        ).astype(jnp.bfloat16),
        "dp",
        scatter_dimension=0,
        tiled=True,
    ).astype(jnp.float32)
    columns = act
    grad_dn = lax.psum_scatter(
        lax.dot_general(
            columns, scaled_dy, (((0,), (0,)), ((), ())), preferred_element_type=jnp.float32
        ).astype(jnp.bfloat16),
        "dp",
        scatter_dimension=0,
        tiled=True,
    ).astype(jnp.float32)
    return (grad_tokens, grad_gates, (grad_gu * grad_scale)[None], (grad_dn * grad_scale)[None])


def solution(mesh):
    in_specs = (
        P(("dp", "expert"), None),
        P(("dp", "expert"), None),
        P(("dp", "expert"), None),
        P(("dp", "expert"), None),
        P("dp", "expert", None, None),
        P("expert", "dp", None),
        P("expert", "dp", None),
    )
    out_specs = (
        P(("dp", "expert"), None),
        P(("dp", "expert"), None),
        P("expert", "dp", None),
        P("expert", "dp", None),
    )
    return jax.shard_map(
        on_device, mesh=mesh, in_specs=in_specs, out_specs=out_specs, check_vma=False
    )
```

profile of v0, /device:TPU:15, one launch (start us, length us, event | category | flops | bytes accessed | tf_op | source)
XLA Modules:
  0.0 384.5 jit_solution(2938252496134357478)
XLA Ops:
  7.2 0.7 all-gather.5.cloned.1.call-update
  7.9 0.7 broadcast_multiply_fusion
  8.6 0.8 copy.18
  9.4 0.1 eq.25
  9.5 0.1 eq.29
  9.7 1.7 reduce-window.6
  11.4 0.3 slice_reduce_fusion
  11.7 0.1 fusion.26
  11.8 0.1 copy.17
  11.9 0.1 mul.76
  12.1 0.8 copy.21
  12.9 0.1 reshape.207
  13.0 8.6 %scatter_custom_fusion = bf16[784]{0:T(1024)(128)(2,1)S(1)} fusion(s32[768]{0:T(1024)S(1)} %fusion.28, bf16[768]{0:T(1024)(128)(2,1)S(1)} %reshape.207, bf16[]{:T(256)} %constant.12.clone.1), kind=kCustom, calls=%fused_computation.64 | custom fusion | bytes 1570 | tf_op jit(solution)/shard_map/scatter | solution.py:27
  21.7 0.7 all_to_all.25
  22.4 7.1 %all-to-all-start = ((bf16[16,1,49]{2,1,0:T(2,128)(2,1)}), bf16[16,1,49]{2,1,0:T(2,128)(2,1)S(1)}, u32[]{:S(2)}, u32[]{:S(2)}) async-start(bf16[16,1,49]{2,1,0:T(2,128)(2,1)} %all_to_all.25), calls=%async_computation | async-start | bytes 16384 | tf_op jit(solution)/shard_map/all_to_all | solution.py:43
  29.5 22.5 %scatter_custom_fusion.1 = bf16[784,2048]{1,0:T(8,128)(2,1)} fusion(s32[768]{0:T(1024)S(1)} %fusion.28, bf16[128,2048]{1,0:T(8,128)(2,1)S(1)} %copy-done, s32[1024]{0:T(1024)S(1)} %pad_clamp_fusion.1, bf16[]{:T(256)} %constant.12.clone.1), kind=kCustom, calls=%fused_computation.21 | custom fusion | bytes 3211266 | tf_op jit(solution)/shard_map/scatter | solution.py:26
  52.0 3.8 reshape.162
  55.8 6.0 %all-to-all-start.1 = ((bf16[16,49,2048]{2,1,0:T(8,128)(2,1)}), bf16[16,49,2048]{2,1,0:T(8,128)(2,1)}, u32[]{:S(2)}, u32[]{:S(2)}) async-start(bf16[16,49,2048]{2,1,0:T(8,128)(2,1)} %reshape.162), calls=%async_computation.1 | async-start | bytes 7340032 | tf_op jit(solution)/shard_map/all_to_all | solution.py:36
  61.8 0.7 all-gather.7.cloned.1.call-update
  62.5 29.5 %scatter_custom_fusion.2 = bf16[784,2048]{1,0:T(8,128)(2,1)S(1)} fusion(s32[768]{0:T(1024)S(1)} %fusion.28, bf16[128,2048]{1,0:T(8,128)(2,1)} %param.7, s32[1024]{0:T(1024)S(1)} %pad_clamp_fusion.1, bf16[]{:T(256)} %constant.12.clone.1), kind=kCustom, calls=%fused_computation.19 | custom fusion | bytes 3211776 | tf_op jit(solution)/shard_map/scatter | solution.py:25
  92.0 2.3 reshape.168
  94.4 48.7 %all-to-all-done.1 = bf16[16,49,2048]{2,1,0:T(8,128)(2,1)} async-done(((bf16[16,49,2048]{2,1,0:T(8,128)(2,1)}), bf16[16,49,2048]{2,1,0:T(8,128)(2,1)}, u32[]{:S(2)}, u32[]{:S(2)}) %all-to-all-start.1) | async-done | bytes 3211296 | tf_op jit(solution)/shard_map/all_to_all | solution.py:36
  143.0 4.9 %all-to-all-start.4 = ((bf16[16,49,2048]{2,1,0:T(8,128)(2,1)}), bf16[16,49,2048]{2,1,0:T(8,128)(2,1)}, u32[]{:S(2)}, u32[]{:S(2)}) async-start(bf16[16,49,2048]{2,1,0:T(8,128)(2,1)} %reshape.168), calls=%async_computation.4 | async-start | bytes 7340032 | tf_op jit(solution)/shard_map/all_to_all | solution.py:29
  147.9 0.2 reduce-scatter.5.cloned.1.call-start
  148.3 2.6 reshape.163
  150.9 7.1 %convolution_convert_fusion.1 = bf16[704,2048]{1,0:T(8,128)(2,1)} fusion(bf16[784,2048]{1,0:T(8,128)(2,1)S(1)} %reshape.163, f32[784]{0:T(1024)S(1)} %reshape.170, bf16[784,1408]{1,0:T(8,128)(2,1)} %bitcast.38), kind=kOutput, calls=%fused_computation.17 | convolution fusion | flops 2271404032 | bytes 8506432 | tf_op jit(solution)/shard_map/dot_general | solution.py:110
  158.1 71.0 %all-to-all-done.4 = bf16[16,49,2048]{2,1,0:T(8,128)(2,1)} async-done(((bf16[16,49,2048]{2,1,0:T(8,128)(2,1)}), bf16[16,49,2048]{2,1,0:T(8,128)(2,1)}, u32[]{:S(2)}, u32[]{:S(2)}) %all-to-all-start.4) | async-done | bytes 3211296 | tf_op jit(solution)/shard_map/all_to_all | solution.py:29
  229.2 3.7 reshape.169
  232.9 6.4 %fusion.14 = (bf16[784,704]{1,0:T(8,128)(2,1)S(1)}, bf16[784,704]{1,0:T(8,128)(2,1)S(1)}, f32[784]{0:T(1024)S(1)}) fusion(f32[784]{0:T(1024)S(1)} %reshape.170, bf16[784,1408]{1,0:T(8,128)(2,1)} %bitcast.39, bf16[784,2048]{1,0:T(8,128)(2,1)S(1)} %reshape.163, bf16[1,704,2048]{2,1,0:T(8,128)(2,1)} %all-gather.5.cloned.1.call-done), kind=kOutput, calls=%fused_computation.30 | convolution fusion | flops 2272871680 | bytes 10516608 | tf_op jit(solution)/shard_map/dot_general | solution.py:55
  239.3 1.0 copy-done.3
  240.3 0.4 copy-done.4
  240.8 8.9 %convolution_convert_fusion = bf16[2048,1408]{1,0:T(8,128)(2,1)} fusion(bf16[784,2048]{1,0:T(8,128)(2,1)S(1)} %copy-done.2, bf16[784,704]{1,0:T(8,128)(2,1)S(1)} %get-tuple-element.13, bf16[784,704]{1,0:T(8,128)(2,1)S(1)} %get-tuple-element.12), kind=kOutput, calls=%fused_computation.7 | convolution fusion | flops 4528758784 | bytes 11186176 | tf_op jit(solution)/shard_map/dot_general | solution.py:101
  249.7 0.7 convert_element_type.86
  250.4 5.2 %all-to-all-start.3 = ((bf16[16,1,49]{2,1,0:T(2,128)(2,1)}), bf16[16,1,49]{2,1,0:T(2,128)(2,1)S(1)}, u32[]{:S(2)}, u32[]{:S(2)}) async-start(bf16[16,1,49]{2,1,0:T(2,128)(2,1)} %convert_element_type.86), calls=%async_computation.3 | async-start | bytes 16384 | tf_op jit(solution)/shard_map/all_to_all | solution.py:83
  255.6 8.5 %fusion.2 = bf16[784,2048]{1,0:T(8,128)(2,1)S(1)} fusion(bf16[1,2048,1408]{2,1,0:T(8,128)(2,1)} %all-gather.7.cloned.1.call-done, bf16[784,704]{1,0:T(8,128)(2,1)} %copy-done.4, bf16[784,704]{1,0:T(8,128)(2,1)} %copy-done.3), kind=kOutput, calls=%fused_computation.16 | convolution fusion | flops 4527480832 | bytes 11186176 | tf_op jit(solution)/shard_map/dot_general | solution.py:69
  264.2 2.4 reshape.164
  266.6 6.0 %all-to-all-start.2 = ((bf16[16,49,2048]{2,1,0:T(8,128)(2,1)}), bf16[16,49,2048]{2,1,0:T(8,128)(2,1)}, u32[]{:S(2)}, u32[]{:S(2)}) async-start(bf16[16,49,2048]{2,1,0:T(8,128)(2,1)} %reshape.164), calls=%async_computation.2 | async-start | bytes 7340032 | tf_op jit(solution)/shard_map/all_to_all | solution.py:76
  272.7 0.1 reshape.166
  272.8 5.0 %gather_fusion.1 = bf16[768]{0:T(1024)(128)(2,1)S(1)} fusion(bf16[784]{0:T(1024)(128)(2,1)S(1)} %reshape.166, s32[1024]{0:T(1024)S(1)} %pad_clamp_fusion), kind=kCustom, calls=%fused_computation.2 | custom fusion | bytes 6144 | tf_op jit(solution)/shard_map/gather | solution.py:97
  277.8 0.1 reshape.167
  277.9 0.7 copy.24
  278.6 3.3 multiply_bitcast_fusion.1
  281.9 72.0 %all-to-all-done.2 = bf16[16,49,2048]{2,1,0:T(8,128)(2,1)} async-done(((bf16[16,49,2048]{2,1,0:T(8,128)(2,1)}), bf16[16,49,2048]{2,1,0:T(8,128)(2,1)}, u32[]{:S(2)}, u32[]{:S(2)}) %all-to-all-start.2) | async-done | bytes 3211296 | tf_op jit(solution)/shard_map/all_to_all | solution.py:76
  353.8 2.6 reshape.165
  356.4 4.3 %gather_fusion = bf16[768,2048]{1,0:T(8,128)(2,1)} fusion(bf16[784,2048]{1,0:T(8,128)(2,1)S(1)} %reshape.165, s32[1024]{0:T(1024)S(1)} %pad_clamp_fusion), kind=kCustom, calls=%fused_computation.1 | custom fusion | bytes 6294528 | tf_op jit(solution)/shard_map/gather | solution.py:92
  360.7 6.3 %gather.16 = bf16[128,6,2048]{2,1,0:T(8,128)(2,1)} reshape(bf16[768,2048]{1,0:T(8,128)(2,1)} %gather_fusion) | data formatting | bytes 6291456 | tf_op jit(solution)/shard_map/gather | solution.py:92
  367.0 5.7 %reduce_sum.34 = bf16[128,2048]{1,0:T(8,128)(2,1)} reduce(bf16[128,6,2048]{2,1,0:T(8,128)(2,1)} %gather.16, bf16[]{:T(256)} %constant.12.clone.1), dimensions={1}, to_apply=%region_5.6 | reduce | flops 1310720 | bytes 3670018 | tf_op jit(solution)/shard_map/reduce_sum | solution.py:96
  372.7 4.9 %multiply_bitcast_fusion = f32[1,1024,1408]{2,1,0:T(8,128)} fusion(bf16[1024,1408]{1,0:T(8,128)(2,1)} %reduce-scatter.3.cloned.1.call-done), kind=kLoop, calls=%fused_computation.11 | loop fusion | flops 2883584 | bytes 8650752 | tf_op jit(solution)/shard_map/broadcast_in_dim | solution.py:117
  (29 shorter events, 0.4 us)
Async XLA Ops:
  7.2 22.4 %copy-start = (bf16[128,2048]{1,0:T(8,128)(2,1)S(1)}, bf16[128,2048]{1,0:T(8,128)(2,1)}, u32[]{:S(2)}) copy-start(bf16[128,2048]{1,0:T(8,128)(2,1)} %param.8) | copy-start | bytes 1572868
  7.2 225.7 %all-gather.5.cloned.1.call-start = ((), (), s32[]{:S(2)}) async-start(), calls=%async_computation.9 | async-start | bytes 4325376 | tf_op jit(solution)/shard_map/all_gather | solution.py:57
  22.4 33.4 %all-to-all-start = ((bf16[16,1,49]{2,1,0:T(2,128)(2,1)}), bf16[16,1,49]{2,1,0:T(2,128)(2,1)S(1)}, u32[]{:S(2)}, u32[]{:S(2)}) async-start(bf16[16,1,49]{2,1,0:T(2,128)(2,1)} %all_to_all.25), calls=%async_computation | async-start | bytes 16384 | tf_op jit(solution)/shard_map/all_to_all | solution.py:43
  55.8 87.2 %all-to-all-start.1 = ((bf16[16,49,2048]{2,1,0:T(8,128)(2,1)}), bf16[16,49,2048]{2,1,0:T(8,128)(2,1)}, u32[]{:S(2)}, u32[]{:S(2)}) async-start(bf16[16,49,2048]{2,1,0:T(8,128)(2,1)} %reshape.162), calls=%async_computation.1 | async-start | bytes 7340032 | tf_op jit(solution)/shard_map/all_to_all | solution.py:36
  61.8 193.8 %all-gather.7.cloned.1.call-start = ((), (), s32[]{:S(2)}) async-start(), calls=%async_computation.10 | async-start | bytes 8650752 | tf_op jit(solution)/shard_map/all_gather | solution.py:71
  143.0 86.1 %all-to-all-start.4 = ((bf16[16,49,2048]{2,1,0:T(8,128)(2,1)}), bf16[16,49,2048]{2,1,0:T(8,128)(2,1)}, u32[]{:S(2)}, u32[]{:S(2)}) async-start(bf16[16,49,2048]{2,1,0:T(8,128)(2,1)} %reshape.168), calls=%async_computation.4 | async-start | bytes 7340032 | tf_op jit(solution)/shard_map/all_to_all | solution.py:29
  147.9 130.6 %reduce-scatter.5.cloned.1.call-start = ((), (), s32[]{:S(2)}) async-start(), calls=%async_computation.8 | async-start | bytes 4325376 | tf_op jit(solution)/shard_map/reduce_scatter | solution.py:109
  158.1 214.6 %reduce-scatter.3.cloned.1.call-start = ((), (), s32[]{:S(2)}) async-start(), calls=%async_computation.7 | async-start | bytes 8650752 | tf_op jit(solution)/shard_map/reduce_scatter | solution.py:100
  232.9 7.9 %copy-start.2 = (bf16[784,2048]{1,0:T(8,128)(2,1)S(1)}, bf16[784,2048]{1,0:T(8,128)(2,1)}, u32[]{:S(2)}) copy-start(bf16[784,2048]{1,0:T(8,128)(2,1)} %reshape.169) | copy-start | bytes 9633796
  239.3 1.0 copy-start.3
  239.3 1.4 copy-start.4
  250.4 16.2 %all-to-all-start.3 = ((bf16[16,1,49]{2,1,0:T(2,128)(2,1)}), bf16[16,1,49]{2,1,0:T(2,128)(2,1)S(1)}, u32[]{:S(2)}, u32[]{:S(2)}) async-start(bf16[16,1,49]{2,1,0:T(2,128)(2,1)} %convert_element_type.86), calls=%async_computation.3 | async-start | bytes 16384 | tf_op jit(solution)/shard_map/all_to_all | solution.py:83
  266.6 87.2 %all-to-all-start.2 = ((bf16[16,49,2048]{2,1,0:T(8,128)(2,1)}), bf16[16,49,2048]{2,1,0:T(8,128)(2,1)}, u32[]{:S(2)}, u32[]{:S(2)}) async-start(bf16[16,49,2048]{2,1,0:T(8,128)(2,1)} %reshape.164), calls=%async_computation.2 | async-start | bytes 7340032 | tf_op jit(solution)/shard_map/all_to_all | solution.py:76
  366.9 10.6 %copy-start.1 = (bf16[128,2048]{1,0:T(8,128)(2,1)S(1)}, bf16[128,2048]{1,0:T(8,128)(2,1)}, u32[]{:S(2)}) copy-start(bf16[128,2048]{1,0:T(8,128)(2,1)} %param.8) | copy-start | bytes 1572868
Sparse Core Ops, SparseCore 0:
  9.6 42.1 all-gather.4
  64.2 74.0 all-gather.6
  158.2 40.0 reduce-scatter.4
  249.8 69.8 reduce-scatter.2
where the time goes:
time: 390 us; the launch traced here: 385 us
  waiting for transfers between devices  193 us (49%)
  local copies, waits for them, and re-layouts  99.8 us (26%)
  matrix products  30.9 us (8%)
  starting transfers between devices  29.7 us (8%)
  other arithmetic  16.5 us (4%)
  between operations  14.4 us (4%)
    all_to_all x1, waiting for transfers between devices, on_device(): lax.all_to_all(row_grad.reshape(experts, capacity, width), 'expert', spli...  72 us
    all_to_all x1, waiting for transfers between devices, on_device(): lax.all_to_all(send_x.reshape(experts, capacity, width), 'expert', split_...  71 us
    scatter x2, local copies, waits for them, and re-layouts, on_device(): jnp.zeros((slot_total, width), jnp.bfloat16).at[slot_index]  52 us
    all_to_all x1, waiting for transfers between devices, on_device(): lax.all_to_all(send_dy.reshape(experts, capacity, width), 'expert', split...  48.7 us
    gather x2, local copies, waits for them, and re-layouts, on_device(): back_rows.reshape(slot_total, width)[slot_index].astype(jnp.float32)  10.5 us
    dot_general x1, matrix products, on_device(): lax.dot_general(columns, pre_grad, (((0,), (0,)), ((), ())), preferred_el...  8.85 us
    scatter x1, local copies, waits for them, and re-layouts, on_device(): jnp.zeros((slot_total,), jnp.bfloat16).at[slot_index]  8.61 us
    dot_general x1, matrix products, on_device(): lax.dot_general(pre_grad, lax.all_gather(gate_up[0], 'dp', axis=0, tiled=...  8.51 us
  transfers between devices with their start and end apart: 9, of which 3 were waited for; matrix products, arithmetic and copies ran while one was open for 36% of the time, Pallas kernels for 0%

commit v1 on v0

v1 whole, which is shorter than its diff:
```python
import jax
import jax.numpy as jnp
import numpy as np
from jax import lax
from jax.sharding import PartitionSpec as P

BF16 = jnp.bfloat16
F32 = jnp.float32


def dot(a, b, contract):
    return lax.dot_general(a, b, (contract, ((), ())), preferred_element_type=F32)


def on_device(tokens, out_grad, routes, gate_weights, saved_preacts, gate_up, down_proj):
    experts = lax.axis_size("expert")
    groups = lax.axis_size("dp")
    tok_rows, top = routes.shape
    width = tokens.shape[1]
    part = width // groups
    slot_total = saved_preacts.shape[2]
    capacity = slot_total // experts
    hidden = saved_preacts.shape[3] // 2
    hidden_part = hidden // groups
    line = 4
    plane = experts // line
    me = lax.axis_index("expert")
    replica = lax.axis_index("dp")
    hi, lo = me // plane, me % plane

    def along_line(v, k):
        if k % line == 0:
            return v
        return lax.ppermute(v, "expert", [(i, (i + k * plane) % experts) for i in range(experts)])

    def in_plane(v, k):
        if k == 0:
            return v
        return lax.ppermute(v, "expert", [(i, i ^ k) for i in range(experts)])

    def over_dp(v, j):
        if j == 0:
            return v
        return lax.ppermute(v, "dp", [(i, (i + j) % groups) for i in range(groups)])

    def part_of(v, index, size, axis):
        return lax.dynamic_slice_in_dim(v, index * size, size, axis)

    def after(v, *others):
        return lax.optimization_barrier((v, *others))[0]

    names = jnp.arange(experts, dtype=jnp.int32)
    hits = routes[:, :, None] == names[None, None, :]
    routed = jnp.any(hits, axis=1)
    gates = jnp.sum(jnp.where(hits, gate_weights.astype(F32)[:, :, None], 0.0), axis=1)
    earlier = np.tril(np.ones((tok_rows, tok_rows), np.float32), -1)
    before = dot(jnp.asarray(earlier, BF16), routed.astype(BF16), ((1,), (0,)))
    places = jnp.where(routed, before + 1.0, 0.0)
    lanes = -(-2 * experts // 128) * 128
    marks = jnp.concatenate([places, gates], axis=1).astype(BF16)
    marks = jnp.pad(marks, ((0, 0), (0, lanes - 2 * experts)))
    lane = jnp.arange(lanes, dtype=jnp.int32)

    piece = -(-line * capacity // 8) * 8
    half = plane // 2 * piece
    inner = np.arange(piece)
    inside = inner < line * capacity
    wanted = np.full((piece, line), -1.0, np.float32)
    wanted[inner[inside], inner[inside] // capacity] = inner[inside] % capacity + 1
    wanted = jnp.asarray(wanted, BF16)
    partner = jnp.arange(plane, dtype=jnp.int32)
    partner_lane = (hi * plane + (lo ^ partner))[:, None] == lane[None, :]
    partner_lane = partner_lane.astype(BF16)

    def picker(held):
        seen = dot(partner_lane, held, ((1,), (1,))).astype(BF16)
        seen = seen.reshape(plane, 1, line, tok_rows)
        hit = seen == wanted[None, :, :, None]
        return hit.astype(BF16).reshape(plane * piece, line * tok_rows)

    def pick(p, held):
        return dot(p, held, ((1,), (0,))).astype(BF16)

    def lines(v):
        return [along_line(v, k) for k in range(line)]

    def stack(values):
        return jnp.concatenate(values, axis=0)

    def block(v, k):
        return v[k * piece : (k + 1) * piece]

    def exchange(v, partners):
        return [in_plane(block(v, k), k) for k in partners]

    everyone = range(plane)

    cols = width // 2
    down_got = [over_dp(down_proj[0], j) for j in range(groups)]
    marks_line = lines(marks)
    dy_first = lines(out_grad[:, :cols])

    step = jnp.asarray(inner // capacity, jnp.int32)
    source = (hi - step) % line * plane + (lo ^ partner[:, None])
    order = jnp.where(jnp.asarray(inside), source * capacity + jnp.asarray(inner % capacity), -1)
    reorder = order.reshape(-1)[:, None] == jnp.arange(slot_total, dtype=jnp.int32)[None, :]
    saved_rows = pick(reorder.astype(BF16), saved_preacts[0, 0])
    held_marks = stack(marks_line)
    own_picker = picker(after(held_marks, saved_rows))

    dy_second = lines(after(out_grad[:, cols:], *dy_first))
    picked_first = pick(after(own_picker, *dy_first), stack(dy_first))
    rows_first = exchange(picked_first, everyone)

    down_got, picked_first = lax.optimization_barrier((down_got, picked_first))
    down_full = jnp.zeros((hidden, width), BF16)
    for j in range(groups):
        down_full = lax.dynamic_update_slice_in_dim(
            down_full, down_got[j], (replica - j) % groups * hidden_part, 0
        )
    x_parts = [part_of(tokens, (replica + j) % groups, part, 1) for j in range(groups)]
    x_others = [
        over_dp(jnp.concatenate([x_parts[j], marks], axis=1), j) for j in range(1, groups)
    ]

    second_in = jnp.concatenate([stack(dy_second), held_marks], axis=1)
    picked_second = pick(after(own_picker, picked_first, down_full), second_in)
    rows_second = exchange(picked_second, everyone)
    x_own_line = lines(after(x_parts[0], *dy_second))

    dy_a = stack(rows_first)
    grad_a = dot(after(dy_a, picked_second), down_full[:, :cols], ((1,), (1,)))
    x_others_line = [lines(after(v, grad_a)) for v in x_others]
    rows_second = stack(rows_second)
    dy_b = rows_second[:, :cols]
    own_lane = (lane == experts + me).astype(F32)
    g_rows = jnp.sum(rows_second[:, cols:].astype(F32) * own_lane, axis=1, keepdims=True)

    def activation(at, previous):
        saved = after(saved_rows, *previous)[at]
        gate_pre = saved[:, :hidden].astype(F32)
        up_pre = saved[:, hidden:].astype(F32)
        sigmoid_gate = jax.nn.sigmoid(gate_pre)
        act = (gate_pre * sigmoid_gate * up_pre).astype(BF16)
        act_grad = grad_a[at] + dot(dy_b[at], down_full[:, cols:], ((1,), (1,)))
        gate_sums = jnp.sum(act.astype(F32) * act_grad, axis=1, keepdims=True)
        gate_sums = (gate_sums / jnp.sqrt(F32(width))).astype(BF16)
        scaled_grad = g_rows[at] * act_grad
        grad_gate = scaled_grad * up_pre * sigmoid_gate * (1.0 + gate_pre * (1.0 - sigmoid_gate))
        grad_up = scaled_grad * gate_pre * sigmoid_gate
        return jnp.concatenate([grad_gate, grad_up], axis=1).astype(BF16), gate_sums, act

    far, far_sums, far_act = activation(slice(half, None), [grad_a])
    near, near_sums, near_act = activation(slice(0, half), [far])

    far_got = [over_dp(far, j) for j in range(1, groups)]
    near_got = [over_dp(after(near, *far_got), j) for j in range(1, groups)]

    def back_rows(v):
        return dot(v, gate_up[0], ((1,), (1,))).astype(BF16)

    def combine(p, back):
        dense = dot(p, back, ((0,), (0,))).astype(BF16)
        return [dense[k * tok_rows : (k + 1) * tok_rows] for k in range(line)]

    def total(values):
        result = values[0].astype(F32)
        for k in range(1, line):
            result = result + along_line(values[k], -k).astype(F32)
        return result

    x_own_line, _ = lax.optimization_barrier((x_own_line, near))
    x_own_picked = pick(own_picker, stack(x_own_line))
    x_own = exchange(x_own_picked, everyone)
    expert_lane = (lane == me).astype(F32)
    own_back = stack([back_rows(after(near, x_own_picked)), back_rows(after(far, x_own_picked))])
    own_sums = stack([near_sums, far_sums]).astype(F32) * expert_lane
    own_back = jnp.concatenate([own_back, own_sums.astype(BF16)], axis=1)
    own_back_got = exchange(own_back, everyone)

    act_late = after(stack([near_act, far_act]), own_back)
    scaled_dy = [(g_rows * v.astype(F32)).astype(BF16) for v in (dy_a, dy_b)]
    grad_dn_full = jnp.concatenate([dot(act_late, v, ((0,), (0,))) for v in scaled_dy], axis=1)

    x_pickers, x_picked = [], []
    for j in range(1, groups):
        held = stack(x_others_line[j - 1])
        x_pickers.append(picker(after(held[:, part:], grad_dn_full)))
        x_picked.append(pick(x_pickers[-1], held[:, :part]))
    far_back = []
    for v in far_got:
        far_rows = back_rows(after(v, *x_picked))
        far_back += [[in_plane(block(far_rows, k - plane // 2), k) for k in everyone if 2 * k >= plane]]
    own_dense = combine(own_picker, after(stack(own_back_got), far_rows))
    own_total = total(own_dense)
    x_other = [exchange(after(v, *far_back[-1]), everyone) for v in x_picked]

    sent = [
        part_of(grad_dn_full, (replica + j) % groups, hidden_part, 0).astype(BF16)
        for j in range(1, groups)
    ]
    sent = [over_dp(after(sent[j - 1], *near_got), j) for j in range(1, groups)]
    others = []
    for j in range(1, groups):
        near_rows = back_rows(after(near_got[j - 1], *far_back[-1], own_dense[0]))
        near_back = [in_plane(block(near_rows, k), k) for k in everyone if 2 * k < plane]
        others.append(combine(x_pickers[j - 1], stack(near_back + far_back[j - 1])))

    grad_scale = 1.0 / jnp.sqrt(F32(groups * tok_rows * top))
    whole = [stack([near, far])] + [stack([a, b]) for a, b in zip(near_got, far_got)]
    x_all = [stack(x_own)] + [stack(v) for v in x_other]
    x_all[0] = after(x_all[0], others[-1][0])
    grad_gu = 0.0
    for x_rows, grads in zip(x_all, whole):
        grad_gu = grad_gu + dot(x_rows, grads, ((0,), (0,)))
    grad_gu = grad_gu * grad_scale

    totals = [after(total(v), *sent) for v in others]
    others = [over_dp(v.astype(BF16), groups - 1 - j) for j, v in enumerate(totals)]
    grad_dn = part_of(grad_dn_full, replica, hidden_part, 0)
    for v in sent:
        grad_dn = grad_dn + v.astype(F32)
    grad_dn = grad_dn * grad_scale

    grad_tokens = jnp.zeros((tok_rows, width), BF16)
    grad_tokens = lax.dynamic_update_slice_in_dim(
        grad_tokens, own_total[:, :part].astype(BF16), replica * part, 1
    )
    for j in range(1, groups):
        grad_tokens = lax.dynamic_update_slice_in_dim(
            grad_tokens, others[j - 1], (replica + j) % groups * part, 1
        )

    found = routes[:, :, None] == names[None, None, :]
    grad_gates = jnp.sum(jnp.where(found, own_total[:, None, part : part + experts], 0.0), axis=2)
    grad_gates = grad_gates.astype(BF16)

    return (grad_tokens, grad_gates, grad_gu[None], grad_dn[None])


def solution(mesh):
    in_specs = (
        P(("dp", "expert"), None),
        P(("dp", "expert"), None),
        P(("dp", "expert"), None),
        P(("dp", "expert"), None),
        P("dp", "expert", None, None),
        P("expert", "dp", None),
        P("expert", "dp", None),
    )
    out_specs = (
        P(("dp", "expert"), None),
        P(("dp", "expert"), None),
        P("expert", "dp", None),
        P("expert", "dp", None),
    )
    return jax.shard_map(
        on_device, mesh=mesh, in_specs=in_specs, out_specs=out_specs, check_vma=False
    )
```

time: 390 us -> 272 us (0.70)
  the two profiles are of different devices: /device:TPU:15 before, /device:TPU:0 now
where the time goes in v1:
time: 272 us; the launch traced here: 271 us
  waiting for transfers between devices  126 us (46%)
  starting transfers between devices  55.9 us (21%)
  matrix products  53.2 us (20%)
  local copies, waits for them, and re-layouts  17.8 us (7%)
  other arithmetic  16.6 us (6%)
    ppermute x21, waiting for transfers between devices, along_line(): lax.ppermute(v, 'expert', [(i, (i + k * plane) % experts) for i in range(...  77.1 us
    dot_general x21, matrix products, dot(): lax.dot_general(a, b, (contract, ((), ())), preferred_element_type=F32)  53.2 us
    ppermute x18, waiting for transfers between devices, in_plane(): return lax.ppermute(v, 'expert', [(i, i ^ k) for i in range(experts)])  43.1 us
    ppermute x21, starting transfers between devices, along_line(): lax.ppermute(v, 'expert', [(i, (i + k * plane) % experts) for i in range(...  39.6 us
    ppermute x18, starting transfers between devices, in_plane(): return lax.ppermute(v, 'expert', [(i, i ^ k) for i in range(experts)])  8.73 us
    ppermute x6, starting transfers between devices, over_dp(): return lax.ppermute(v, 'dp', [(i, (i + j) % groups) for i in range(groups)])  7.54 us
    ppermute x6, waiting for transfers between devices, over_dp(): return lax.ppermute(v, 'dp', [(i, (i + j) % groups) for i in range(groups)])  5.67 us
  transfers between devices with their start and end apart: 45, of which 18 were waited for; matrix products, arithmetic and copies ran while one was open for 27% of the time, Pallas kernels for 0%

profile of v1, /device:TPU:0, one launch (start us, length us, event | category | flops | bytes accessed | tf_op | source)
XLA Modules:
  0.0 270.9 jit_solution(3056892838978167749)
XLA Ops:
  3.8 5.1 %collective-permute-start.2 = (bf16[128,128]{0,1:T(8,128)(2,1)S(1)}, bf16[128,128]{0,1:T(8,128)(2,1)S(1)}, u32[]{:S(2)}, u32[]{:S(2)}) collective-permute-start(bf16[128,128]{0,1:T(8,128)(2,1)S(1)} %fusion.125), channel_id=1, source_target_pairs={{0,12},{1,13},{2,14},{3,15},{4,0},{5,1},{6,2},{7,3},{8,4},{9,5},{1... | collective-permute-start | bytes 98312 | tf_op jit(solution)/shard_map/ppermute | solution.py:34
  9.9 1.8 fusion.150
  11.7 2.8 %collective-permute-start.6 = (bf16[128,1024]{1,0:T(8,128)(2,1)S(1)}, bf16[128,1024]{1,0:T(8,128)(2,1)}, u32[]{:S(2)}, u32[]{:S(2)}) collective-permute-start(bf16[128,1024]{1,0:T(8,128)(2,1)S(1)} %get-tuple-element.103), channel_id=1, source_target_pairs={{0,12},{1,13},{2,14},{3,15},{4,0},{5,1},{6,2},{7,3},{8,4},{9,5},{1... | collective-permute-start | bytes 786440 | tf_op jit(solution)/shard_map/ppermute | solution.py:34
  17.2 5.8 %convolution_convert_fusion.1 = bf16[800,1408]{1,0:T(8,128)(2,1)} fusion(bf16[1,1,784,1408]{3,2,1,0:T(8,128)(2,1)} %param.16, s32[800]{0:T(1024)S(1)} %select_n.86), kind=kOutput, calls=%fused_computation.7 | convolution fusion | flops 1767948800 | bytes 4463744 | tf_op jit(solution)/shard_map/dot_general | solution.py:12
  23.7 1.6 collective-permute-start.3
  27.7 10.1 %collective-permute-done.5 = bf16[128,1024]{1,0:T(8,128)(2,1)} collective-permute-done((bf16[128,1024]{1,0:T(8,128)(2,1)S(1)}, bf16[128,1024]{1,0:T(8,128)(2,1)}, u32[]{:S(2)}, u32[]{:S(2)}) %collective-permute-start.5) | collective-permute-done | bytes 262176 | tf_op jit(solution)/shard_map/ppermute | solution.py:34
  37.8 1.5 collective-permute-start.8
  39.3 2.1 convolution_convert_fusion.5
  45.5 11.2 %collective-permute-done.8 = bf16[128,1024]{1,0:T(8,128)(2,1)} collective-permute-done((bf16[128,1024]{1,0:T(8,128)(2,1)}, bf16[128,1024]{1,0:T(8,128)(2,1)}, u32[]{:S(2)}, u32[]{:S(2)}) %collective-permute-start.8) | collective-permute-done | bytes 262176 | tf_op jit(solution)/shard_map/ppermute | solution.py:34
  58.6 1.5 pad_maximum_fusion.18
  61.1 4.6 %collective-permute-done.7 = bf16[128,1024]{1,0:T(8,128)(2,1)} collective-permute-done((bf16[128,1024]{1,0:T(8,128)(2,1)}, bf16[128,1024]{1,0:T(8,128)(2,1)}, u32[]{:S(2)}, u32[]{:S(2)}) %collective-permute-start.7) | collective-permute-done | bytes 262176 | tf_op jit(solution)/shard_map/ppermute | solution.py:34
  65.7 1.6 collective-permute-start.23
  70.7 1.6 constant_dynamic-update-slice_fusion.5
  72.4 3.2 %convolution_convert_fusion = bf16[800,1152]{1,0:T(8,128)(2,1)S(1)} fusion(bf16[800,512]{1,0:T(8,128)(2,1)S(1)} %copy-done.14, bf16[512,128]{1,0:T(8,128)(2,1)S(1)} %copy.20, bf16[128,1024]{1,0:T(8,128)(2,1)} %collective-permute-done.9, bf16[128,1024]{1,0:T(8,128)(2,1)} %collective-permute-done.8, bf16[128,1024]{1,0:T(8,128)(2,1)} %collective-permute-done.7, ...), kind=kOutput, calls=%fused_computation.6 | convolution fusion | flops 950538240 | bytes 3842048 | tf_op jit(solution)/shard_map/dot_general | solution.py:12
  75.6 2.9 %fusion.51 = f32[800,704]{1,0:T(8,128)} fusion(bf16[800,1024]{1,0:T(8,128)(2,1)S(1)} %pad_maximum_fusion.9, bf16[704,2048]{1,0:T(8,128)(2,1)S(1)} %constant_dynamic-update-slice_fusion.5), kind=kOutput, calls=%fused_computation.82 | convolution fusion | flops 1153433600 | bytes 5332992 | tf_op jit(solution)/shard_map/dot_general | solution.py:12
  78.6 3.9 %collective-permute-start.26 = (bf16[128,1152]{1,0:T(8,128)(2,1)S(1)}, bf16[128,1152]{1,0:T(8,128)(2,1)S(1)}, u32[]{:S(2)}, u32[]{:S(2)}) collective-permute-start(bf16[128,1152]{1,0:T(8,128)(2,1)S(1)} %collective-permute-done.23), channel_id=1, source_target_pairs={{0,12},{1,13},{2,14},{3,15},{4,0},{5,1},{6,2},{7,3},{8,4},{9,5},{1... | collective-permute-start | bytes 884744 | tf_op jit(solution)/shard_map/ppermute | solution.py:34
  84.7 16.2 %collective-permute-done.24 = bf16[128,1152]{1,0:T(8,128)(2,1)S(1)} collective-permute-done((bf16[128,1152]{1,0:T(8,128)(2,1)S(1)}, bf16[128,1152]{1,0:T(8,128)(2,1)S(1)}, u32[]{:S(2)}, u32[]{:S(2)}) %collective-permute-start.24) | collective-permute-done | bytes 294944 | tf_op jit(solution)/shard_map/ppermute | solution.py:34
  100.9 7.3 %collective-permute-done.25 = bf16[128,1152]{1,0:T(8,128)(2,1)S(1)} collective-permute-done((bf16[128,1152]{1,0:T(8,128)(2,1)S(1)}, bf16[128,1152]{1,0:T(8,128)(2,1)S(1)}, u32[]{:S(2)}, u32[]{:S(2)}) %collective-permute-start.25) | collective-permute-done | bytes 294944 | tf_op jit(solution)/shard_map/ppermute | solution.py:34
  108.2 1.5 collective-permute-start.11
  111.8 3.6 %convolution_convert_fusion.3 = bf16[800,1024]{1,0:T(8,128)(2,1)} fusion(pred[100,8,4,128]{3,2,1,0:T(4,128)(4,1)S(1)} %bitcast.70, bf16[512,1152]{1,0:T(8,128)(2,1)} %copy-done.25), kind=kOutput, calls=%fused_computation.44 | convolution fusion | flops 839680000 | bytes 3096576 | tf_op jit(solution)/shard_map/dot_general | solution.py:12
  115.4 7.6 %collective-permute-start.16 = (bf16[128,1024]{1,0:T(8,128)(2,1)S(1)}, bf16[128,1024]{1,0:T(8,128)(2,1)S(1)}, u32[]{:S(2)}, u32[]{:S(2)}) collective-permute-start(bf16[128,1024]{1,0:T(8,128)(2,1)S(1)} %copy-done.22), channel_id=1, source_target_pairs={{0,4},{1,5},{2,6},{3,7},{4,8},{5,9},{6,10},{7,11},{8,12},{9,13},{1... | collective-permute-start | bytes 786440 | tf_op jit(solution)/shard_map/ppermute | solution.py:34
  125.1 2.8 %fusion.72 = (bf16[400,704]{1,0:T(8,128)(2,1)S(1)}, bf16[400,704]{1,0:T(8,128)(2,1)S(1)}, f32[400]{0:T(512)S(1)}, bf16[400,704]{1,0:T(8,128)(2,1)S(1)}) fusion(f32[400]{0:T(512)S(1)} %get-tuple-element.105, bf16[800,1408]{1,0:T(8,128)(2,1)S(1)} %copy-done.40, bf16[704,2048]{1,0:T(8,128)(2,1)S(1)} %copy-done.6, ...), kind=kOutput, calls=%fused_computation.97 | convolution fusion | flops 584831616 | bytes 6514240 | tf_op jit(solution)/shard_map/dot_general | solution.py:12
  128.2 2.6 fusion.76
  131.8 2.0 convolution_convert_fusion.4
  140.6 3.0 %fusion.23 = f32[704,1024]{1,0:T(8,128)S(1)} fusion(bf16[800,704]{1,0:T(8,128)(2,1)S(1)} %pad_maximum_fusion.11, bf16[200,1152]{1,0:T(8,128)(2,1)} %collective-permute-done.12, bf16[200,1152]{1,0:T(8,128)(2,1)} %collective-permute-done.11, bf16[200,1152]{1,0:T(8,128)(2,1)} %collective-permute-done.10, bf16[200,1152]{1,0:T(8,128)(2,1)S(1)} %get-tuple-element.74, ...), kind=kOutput, calls=%fused_computation.48 | convolution fusion | flops 1161625600 | bytes 5856384 | tf_op jit(solution)/shard_map/dot_general | solution.py:12
  143.6 6.5 %collective-permute-done.41 = bf16[200,1024]{1,0:T(8,128)(2,1)S(1)} collective-permute-done((bf16[200,1024]{1,0:T(8,128)(2,1)S(1)}, bf16[200,1024]{1,0:T(8,128)(2,1)S(1)}, u32[]{:S(2)}, u32[]{:S(2)}) %collective-permute-start.41) | collective-permute-done | bytes 409632 | tf_op jit(solution)/shard_map/ppermute | solution.py:39
  150.7 8.1 %collective-permute-done.40 = bf16[200,1024]{1,0:T(8,128)(2,1)S(1)} collective-permute-done((bf16[200,1024]{1,0:T(8,128)(2,1)S(1)}, bf16[200,1024]{1,0:T(8,128)(2,1)S(1)}, u32[]{:S(2)}, u32[]{:S(2)}) %collective-permute-start.40) | collective-permute-done | bytes 409632 | tf_op jit(solution)/shard_map/ppermute | solution.py:39
  159.0 3.1 %fusion.22 = f32[704,1024]{1,0:T(8,128)S(1)} fusion(bf16[800,704]{1,0:T(8,128)(2,1)S(1)} %pad_maximum_fusion.11, f32[800]{0:T(1024)S(1)} %multiply_reduce_fusion.2, bf16[200,1024]{1,0:T(8,128)(2,1)} %collective-permute-done.15, bf16[200,1024]{1,0:T(8,128)(2,1)} %collective-permute-done.14, bf16[200,1024]{1,0:T(8,128)(2,1)} %collective-permute-done.13, ...), kind=kOutput, calls=%fused_computation.47 | convolution fusion | flops 1161625600 | bytes 5651584 | tf_op jit(solution)/shard_map/dot_general | solution.py:12
  162.1 1.5 fusion.1
  164.3 4.5 %collective-permute-done.21 = bf16[200,1152]{1,0:T(8,128)(2,1)S(1)} collective-permute-done((bf16[200,1152]{1,0:T(8,128)(2,1)S(1)}, bf16[200,1152]{1,0:T(8,128)(2,1)S(1)}, u32[]{:S(2)}, u32[]{:S(2)}) %collective-permute-start.21) | collective-permute-done | bytes 460832 | tf_op jit(solution)/shard_map/ppermute | solution.py:39
  168.8 9.8 %collective-permute-done.20 = bf16[200,1152]{1,0:T(8,128)(2,1)S(1)} collective-permute-done((bf16[200,1152]{1,0:T(8,128)(2,1)S(1)}, bf16[200,1152]{1,0:T(8,128)(2,1)S(1)}, u32[]{:S(2)}, u32[]{:S(2)}) %collective-permute-start.20) | collective-permute-done | bytes 460832 | tf_op jit(solution)/shard_map/ppermute | solution.py:39
  178.8 1.7 fusion.60
  180.5 1.6 collective-permute-start.30
  182.0 1.6 convolution_convert_fusion.2
  184.0 8.7 %collective-permute-start.29 = (bf16[128,1152]{1,0:T(8,128)(2,1)S(1)}, bf16[128,1152]{1,0:T(8,128)(2,1)S(1)}, u32[]{:S(2)}, u32[]{:S(2)}) collective-permute-start(bf16[128,1152]{1,0:T(8,128)(2,1)S(1)} %get-tuple-element.91), channel_id=1, source_target_pairs={{0,4},{1,5},{2,6},{3,7},{4,8},{5,9},{6,10},{7,11},{8,12},{9,13},{1... | collective-permute-start | bytes 884744 | tf_op jit(solution)/shard_map/ppermute | solution.py:34
  192.7 3.9 %collective-permute-start.28 = (bf16[128,1152]{1,0:T(8,128)(2,1)S(1)}, bf16[128,1152]{1,0:T(8,128)(2,1)S(1)}, u32[]{:S(2)}, u32[]{:S(2)}) collective-permute-start(bf16[128,1152]{1,0:T(8,128)(2,1)S(1)} %get-tuple-element.92), channel_id=1, source_target_pairs={{0,8},{1,9},{2,10},{3,11},{4,12},{5,13},{6,14},{7,15},{8,0},{9,1},... | collective-permute-start | bytes 884744 | tf_op jit(solution)/shard_map/ppermute | solution.py:34
  196.6 5.2 %fusion.14 = f32[1024,1408]{1,0:T(8,128)} fusion(bf16[800,1024]{1,0:T(8,128)(2,1)S(1)} %pad_maximum_fusion.10, bf16[400,1408]{1,0:T(8,128)(2,1)S(1)} %pad_maximum_fusion.12, bf16[400,1408]{1,0:T(8,128)(2,1)S(1)} %pad_maximum_fusion.13), kind=kOutput, calls=%fused_computation.26 | convolution fusion | flops 2311372800 | bytes 9658368 | tf_op jit(solution)/shard_map/dot_general | solution.py:12
  202.4 8.0 %collective-permute-done.29 = bf16[128,1152]{1,0:T(8,128)(2,1)S(1)} collective-permute-done((bf16[128,1152]{1,0:T(8,128)(2,1)S(1)}, bf16[128,1152]{1,0:T(8,128)(2,1)S(1)}, u32[]{:S(2)}, u32[]{:S(2)}) %collective-permute-start.29) | collective-permute-done | bytes 294944 | tf_op jit(solution)/shard_map/ppermute | solution.py:34
  210.4 10.2 %collective-permute-done.28 = bf16[128,1152]{1,0:T(8,128)(2,1)S(1)} collective-permute-done((bf16[128,1152]{1,0:T(8,128)(2,1)S(1)}, bf16[128,1152]{1,0:T(8,128)(2,1)S(1)}, u32[]{:S(2)}, u32[]{:S(2)}) %collective-permute-start.28) | collective-permute-done | bytes 294944 | tf_op jit(solution)/shard_map/ppermute | solution.py:34
  224.3 1.8 fusion.143
  226.2 1.9 collective-permute-start.43
  229.3 2.5 fusion.46
  233.0 4.5 %collective-permute-done.44 = bf16[200,1024]{1,0:T(8,128)(2,1)S(1)} collective-permute-done((bf16[200,1024]{1,0:T(8,128)(2,1)S(1)}, bf16[200,1024]{1,0:T(8,128)(2,1)S(1)}, u32[]{:S(2)}, u32[]{:S(2)}) %collective-permute-start.44) | collective-permute-done | bytes 409632 | tf_op jit(solution)/shard_map/ppermute | solution.py:39
  238.0 8.7 %collective-permute-done.43 = bf16[200,1024]{1,0:T(8,128)(2,1)S(1)} collective-permute-done((bf16[200,1024]{1,0:T(8,128)(2,1)S(1)}, bf16[200,1024]{1,0:T(8,128)(2,1)S(1)}, u32[]{:S(2)}, u32[]{:S(2)}) %collective-permute-start.43) | collective-permute-done | bytes 409632 | tf_op jit(solution)/shard_map/ppermute | solution.py:39
  247.0 5.5 %multiply_bitcast_fusion = f32[1,1024,1408]{2,1,0:T(8,128)} fusion(f32[1024,1408]{1,0:T(8,128)S(1)} %bitcast.64, bf16[400,1408]{1,0:T(8,128)(2,1)S(1)} %copy-done.32, bf16[400,1408]{1,0:T(8,128)(2,1)S(1)} %copy-done.34, bf16[200,1024]{1,0:T(8,128)(2,1)S(1)} %collective-permute-done.44, bf16[200,1024]{1,0:T(8,128)(2,1)S(1)} %collective-permute-done.43, ...), kind=kOutput, calls=%fused_computation.5 | convolution fusion | flops 2320809984 | bytes 15425536 | tf_op jit(solution)/shard_map/dot_general | solution.py:12
  252.5 8.5 %collective-permute-done.35 = bf16[128,1024]{1,0:T(8,128)(2,1)S(1)} collective-permute-done((bf16[128,1024]{1,0:T(8,128)(2,1)S(1)}, bf16[128,1024]{1,0:T(8,128)(2,1)S(1)}, u32[]{:S(2)}, u32[]{:S(2)}) %collective-permute-start.35) | collective-permute-done | bytes 262176 | tf_op jit(solution)/shard_map/ppermute | solution.py:34
  263.2 2.0 fusion.5
  265.2 4.8 %collective-permute-done.38 = bf16[128,1024]{1,0:T(8,128)(2,1)S(1)} collective-permute-done((bf16[128,1024]{1,0:T(8,128)(2,1)S(1)}, bf16[128,1024]{1,0:T(8,128)(2,1)S(1)}, u32[]{:S(2)}, u32[]{:S(2)}) %collective-permute-start.38) | collective-permute-done | bytes 262176 | tf_op jit(solution)/shard_map/ppermute | solution.py:44
  (211 shorter events, 46.8 us)
Async XLA Ops:
  0.6 134.0 %copy-start = (bf16[1,1024,1408]{2,1,0:T(8,128)(2,1)S(1)}, bf16[1,1024,1408]{2,1,0:T(8,128)(2,1)}, u32[]{:S(2)}) copy-start(bf16[1,1024,1408]{2,1,0:T(8,128)(2,1)} %param.17) | copy-start | bytes 8650756
  3.8 19.9 %collective-permute-start.2 = (bf16[128,128]{0,1:T(8,128)(2,1)S(1)}, bf16[128,128]{0,1:T(8,128)(2,1)S(1)}, u32[]{:S(2)}, u32[]{:S(2)}) collective-permute-start(bf16[128,128]{0,1:T(8,128)(2,1)S(1)} %fusion.125), channel_id=1, source_target_pairs={{0,12},{1,13},{2,14},{3,15},{4,0},{5,1},{6,2},{7,3},{8,4},{9,5},{1... | collective-permute-start | bytes 98312 | tf_op jit(solution)/shard_map/ppermute | solution.py:34
  8.9 14.8 %collective-permute-start.1 = (bf16[128,128]{0,1:T(8,128)(2,1)S(1)}, bf16[128,128]{0,1:T(8,128)(2,1)}, u32[]{:S(2)}, u32[]{:S(2)}) collective-permute-start(bf16[128,128]{0,1:T(8,128)(2,1)S(1)} %fusion.125), channel_id=1, source_target_pairs={{0,8},{1,9},{2,10},{3,11},{4,12},{5,13},{6,14},{7,15},{8,0},{9,1},... | collective-permute-start | bytes 98312 | tf_op jit(solution)/shard_map/ppermute | solution.py:34
  8.9 16.4 %collective-permute-start = (bf16[128,128]{0,1:T(8,128)(2,1)S(1)}, bf16[128,128]{0,1:T(8,128)(2,1)}, u32[]{:S(2)}, u32[]{:S(2)}) collective-permute-start(bf16[128,128]{0,1:T(8,128)(2,1)S(1)} %fusion.125), channel_id=1, source_target_pairs={{0,4},{1,5},{2,6},{3,7},{4,8},{5,9},{6,10},{7,11},{8,12},{9,13},{1... | collective-permute-start | bytes 98312 | tf_op jit(solution)/shard_map/ppermute | solution.py:34
  11.7 16.0 %collective-permute-start.6 = (bf16[128,1024]{1,0:T(8,128)(2,1)S(1)}, bf16[128,1024]{1,0:T(8,128)(2,1)}, u32[]{:S(2)}, u32[]{:S(2)}) collective-permute-start(bf16[128,1024]{1,0:T(8,128)(2,1)S(1)} %get-tuple-element.103), channel_id=1, source_target_pairs={{0,12},{1,13},{2,14},{3,15},{4,0},{5,1},{6,2},{7,3},{8,4},{9,5},{1... | collective-permute-start | bytes 786440 | tf_op jit(solution)/shard_map/ppermute | solution.py:34
  14.5 23.3 %collective-permute-start.5 = (bf16[128,1024]{1,0:T(8,128)(2,1)S(1)}, bf16[128,1024]{1,0:T(8,128)(2,1)}, u32[]{:S(2)}, u32[]{:S(2)}) collective-permute-start(bf16[128,1024]{1,0:T(8,128)(2,1)S(1)} %get-tuple-element.103), channel_id=1, source_target_pairs={{0,8},{1,9},{2,10},{3,11},{4,12},{5,13},{6,14},{7,15},{8,0},{9,1},... | collective-permute-start | bytes 786440 | tf_op jit(solution)/shard_map/ppermute | solution.py:34
  23.7 14.1 %collective-permute-start.4 = (bf16[128,1024]{1,0:T(8,128)(2,1)S(1)}, bf16[128,1024]{1,0:T(8,128)(2,1)}, u32[]{:S(2)}, u32[]{:S(2)}) collective-permute-start(bf16[128,1024]{1,0:T(8,128)(2,1)S(1)} %get-tuple-element.103), channel_id=1, source_target_pairs={{0,4},{1,5},{2,6},{3,7},{4,8},{5,9},{6,10},{7,11},{8,12},{9,13},{1... | collective-permute-start | bytes 786440 | tf_op jit(solution)/shard_map/ppermute | solution.py:34
  23.7 45.5 %collective-permute-start.3 = (bf16[352,2048]{1,0:T(8,128)(2,1)}, bf16[352,2048]{1,0:T(8,128)(2,1)}, u32[]{:S(2)}, u32[]{:S(2)}) collective-permute-start(bf16[352,2048]{1,0:T(8,128)(2,1)} %bitcast.68), channel_id=1, source_target_pairs={{0,16},{16,0},{1,17},{17,1},{2,18},{18,2},{3,19},{19,3},{4,20},{20... | collective-permute-start | bytes 4325384 | tf_op jit(solution)/shard_map/ppermute | solution.py:44
  37.8 7.1 %collective-permute-start.9 = (bf16[128,1024]{1,0:T(8,128)(2,1)}, bf16[128,1024]{1,0:T(8,128)(2,1)}, u32[]{:S(2)}, u32[]{:S(2)}) collective-permute-start(bf16[128,1024]{1,0:T(8,128)(2,1)} %get-tuple-element.36), channel_id=1, source_target_pairs={{0,12},{1,13},{2,14},{3,15},{4,0},{5,1},{6,2},{7,3},{8,4},{9,5},{1... | collective-permute-start | bytes 786440 | tf_op jit(solution)/shard_map/ppermute | solution.py:34
  37.8 18.8 %collective-permute-start.8 = (bf16[128,1024]{1,0:T(8,128)(2,1)}, bf16[128,1024]{1,0:T(8,128)(2,1)}, u32[]{:S(2)}, u32[]{:S(2)}) collective-permute-start(bf16[128,1024]{1,0:T(8,128)(2,1)} %get-tuple-element.36), channel_id=1, source_target_pairs={{0,8},{1,9},{2,10},{3,11},{4,12},{5,13},{6,14},{7,15},{8,0},{9,1},... | collective-permute-start | bytes 786440 | tf_op jit(solution)/shard_map/ppermute | solution.py:34
  42.5 26.7 %copy-start.7 = (bf16[200,1024]{1,0:T(8,128)(2,1)}, bf16[200,1024]{1,0:T(8,128)(2,1)S(1)}, u32[]{:S(2)}) copy-start(bf16[200,1024]{1,0:T(8,128)(2,1)S(1)} %get-tuple-element.86) | copy-start | bytes 1228804
  42.5 24.8 %collective-permute-start.15 = (bf16[200,1024]{1,0:T(8,128)(2,1)}, bf16[200,1024]{1,0:T(8,128)(2,1)}, u32[]{:S(2)}, u32[]{:S(2)}) collective-permute-start(bf16[200,1024]{1,0:T(8,128)(2,1)} %get-tuple-element.87), channel_id=1, source_target_pairs={{0,3},{1,2},{2,1},{3,0},{4,7},{5,6},{6,5},{7,4},{8,11},{9,10},{10,... | collective-permute-start | bytes 1228808 | tf_op jit(solution)/shard_map/ppermute | solution.py:39
  42.7 25.1 %collective-permute-start.14 = (bf16[200,1024]{1,0:T(8,128)(2,1)}, bf16[200,1024]{1,0:T(8,128)(2,1)}, u32[]{:S(2)}, u32[]{:S(2)}) collective-permute-start(bf16[200,1024]{1,0:T(8,128)(2,1)} %get-tuple-element.88), channel_id=1, source_target_pairs={{0,2},{1,3},{2,0},{3,1},{4,6},{5,7},{6,4},{7,5},{8,10},{9,11},{10,... | collective-permute-start | bytes 1228808 | tf_op jit(solution)/shard_map/ppermute | solution.py:39
  44.9 22.9 %collective-permute-start.13 = (bf16[200,1024]{1,0:T(8,128)(2,1)}, bf16[200,1024]{1,0:T(8,128)(2,1)}, u32[]{:S(2)}, u32[]{:S(2)}) collective-permute-start(bf16[200,1024]{1,0:T(8,128)(2,1)} %get-tuple-element.89), channel_id=1, source_target_pairs={{0,1},{1,0},{2,3},{3,2},{4,5},{5,4},{6,7},{7,6},{8,9},{9,8},{10,11... | collective-permute-start | bytes 1228808 | tf_op jit(solution)/shard_map/ppermute | solution.py:39
  56.7 9.0 %collective-permute-start.7 = (bf16[128,1024]{1,0:T(8,128)(2,1)}, bf16[128,1024]{1,0:T(8,128)(2,1)}, u32[]{:S(2)}, u32[]{:S(2)}) collective-permute-start(bf16[128,1024]{1,0:T(8,128)(2,1)} %get-tuple-element.36), channel_id=1, source_target_pairs={{0,4},{1,5},{2,6},{3,7},{4,8},{5,9},{6,10},{7,11},{8,12},{9,13},{1... | collective-permute-start | bytes 786440 | tf_op jit(solution)/shard_map/ppermute | solution.py:34
  65.7 12.9 %collective-permute-start.23 = (bf16[128,1152]{1,0:T(8,128)(2,1)}, bf16[128,1152]{1,0:T(8,128)(2,1)S(1)}, u32[]{:S(2)}, u32[]{:S(2)}) collective-permute-start(bf16[128,1152]{1,0:T(8,128)(2,1)} %pad_maximum_fusion.18), channel_id=1, source_target_pairs={{0,16},{16,0},{1,17},{17,1},{2,18},{18,2},{3,19},{19,3},{4,20},{20... | collective-permute-start | bytes 884744 | tf_op jit(solution)/shard_map/ppermute | solution.py:44
  67.3 63.9 %collective-permute-start.18 = (bf16[128,1024]{1,0:T(8,128)(2,1)}, bf16[128,1024]{1,0:T(8,128)(2,1)}, u32[]{:S(2)}, u32[]{:S(2)}) collective-permute-start(bf16[128,1024]{1,0:T(8,128)(2,1)} %get-tuple-element.41), channel_id=1, source_target_pairs={{0,12},{1,13},{2,14},{3,15},{4,0},{5,1},{6,2},{7,3},{8,4},{9,5},{1... | collective-permute-start | bytes 786440 | tf_op jit(solution)/shard_map/ppermute | solution.py:34
  67.8 63.4 %collective-permute-start.17 = (bf16[128,1024]{1,0:T(8,128)(2,1)}, bf16[128,1024]{1,0:T(8,128)(2,1)}, u32[]{:S(2)}, u32[]{:S(2)}) collective-permute-start(bf16[128,1024]{1,0:T(8,128)(2,1)} %get-tuple-element.41), channel_id=1, source_target_pairs={{0,8},{1,9},{2,10},{3,11},{4,12},{5,13},{6,14},{7,15},{8,0},{9,1},... | collective-permute-start | bytes 786440 | tf_op jit(solution)/shard_map/ppermute | solution.py:34
  78.6 31.2 %collective-permute-start.26 = (bf16[128,1152]{1,0:T(8,128)(2,1)S(1)}, bf16[128,1152]{1,0:T(8,128)(2,1)S(1)}, u32[]{:S(2)}, u32[]{:S(2)}) collective-permute-start(bf16[128,1152]{1,0:T(8,128)(2,1)S(1)} %collective-permute-done.23), channel_id=1, source_target_pairs={{0,12},{1,13},{2,14},{3,15},{4,0},{5,1},{6,2},{7,3},{8,4},{9,5},{1... | collective-permute-start | bytes 884744 | tf_op jit(solution)/shard_map/ppermute | solution.py:34
  82.4 25.8 %collective-permute-start.25 = (bf16[128,1152]{1,0:T(8,128)(2,1)S(1)}, bf16[128,1152]{1,0:T(8,128)(2,1)S(1)}, u32[]{:S(2)}, u32[]{:S(2)}) collective-permute-start(bf16[128,1152]{1,0:T(8,128)(2,1)S(1)} %collective-permute-done.23), channel_id=1, source_target_pairs={{0,8},{1,9},{2,10},{3,11},{4,12},{5,13},{6,14},{7,15},{8,0},{9,1},... | collective-permute-start | bytes 884744 | tf_op jit(solution)/shard_map/ppermute | solution.py:34
  82.4 18.4 %collective-permute-start.24 = (bf16[128,1152]{1,0:T(8,128)(2,1)S(1)}, bf16[128,1152]{1,0:T(8,128)(2,1)S(1)}, u32[]{:S(2)}, u32[]{:S(2)}) collective-permute-start(bf16[128,1152]{1,0:T(8,128)(2,1)S(1)} %collective-permute-done.23), channel_id=1, source_target_pairs={{0,4},{1,5},{2,6},{3,7},{4,8},{5,9},{6,10},{7,11},{8,12},{9,13},{1... | collective-permute-start | bytes 884744 | tf_op jit(solution)/shard_map/ppermute | solution.py:34
  84.6 26.5 %copy-start.24 = (bf16[200,4]{1,0:T(8,128)(2,1)S(1)}, bf16[200,4]{1,0:T(8,128)(2,1)}, u32[]{:S(2)}) copy-start(bf16[200,4]{1,0:T(8,128)(2,1)} %constant.111.clone) | copy-start | bytes 4804
  100.9 14.5 %collective-permute-start.12 = (bf16[200,1152]{1,0:T(8,128)(2,1)}, bf16[200,1152]{1,0:T(8,128)(2,1)}, u32[]{:S(2)}, u32[]{:S(2)}) collective-permute-start(bf16[200,1152]{1,0:T(8,128)(2,1)} %get-tuple-element.75), channel_id=1, source_target_pairs={{0,3},{1,2},{2,1},{3,0},{4,7},{5,6},{6,5},{7,4},{8,11},{9,10},{10,... | collective-permute-start | bytes 1382408 | tf_op jit(solution)/shard_map/ppermute | solution.py:39
  108.2 15.7 %collective-permute-start.11 = (bf16[200,1152]{1,0:T(8,128)(2,1)}, bf16[200,1152]{1,0:T(8,128)(2,1)}, u32[]{:S(2)}, u32[]{:S(2)}) collective-permute-start(bf16[200,1152]{1,0:T(8,128)(2,1)} %get-tuple-element.76), channel_id=1, source_target_pairs={{0,2},{1,3},{2,0},{3,1},{4,6},{5,7},{6,4},{7,5},{8,10},{9,11},{10,... | collective-permute-start | bytes 1382408 | tf_op jit(solution)/shard_map/ppermute | solution.py:39
  109.8 14.2 %collective-permute-start.10 = (bf16[200,1152]{1,0:T(8,128)(2,1)}, bf16[200,1152]{1,0:T(8,128)(2,1)}, u32[]{:S(2)}, u32[]{:S(2)}) collective-permute-start(bf16[200,1152]{1,0:T(8,128)(2,1)} %get-tuple-element.77), channel_id=1, source_target_pairs={{0,1},{1,0},{2,3},{3,2},{4,5},{5,4},{6,7},{7,6},{8,9},{9,8},{10,11... | collective-permute-start | bytes 1382408 | tf_op jit(solution)/shard_map/ppermute | solution.py:39
  115.4 15.8 %collective-permute-start.16 = (bf16[128,1024]{1,0:T(8,128)(2,1)S(1)}, bf16[128,1024]{1,0:T(8,128)(2,1)S(1)}, u32[]{:S(2)}, u32[]{:S(2)}) collective-permute-start(bf16[128,1024]{1,0:T(8,128)(2,1)S(1)} %copy-done.22), channel_id=1, source_target_pairs={{0,4},{1,5},{2,6},{3,7},{4,8},{5,9},{6,10},{7,11},{8,12},{9,13},{1... | collective-permute-start | bytes 786440 | tf_op jit(solution)/shard_map/ppermute | solution.py:34
  133.9 44.9 %collective-permute-start.22 = (bf16[400,1408]{1,0:T(8,128)(2,1)S(1)}, bf16[400,1408]{1,0:T(8,128)(2,1)S(1)}, u32[]{:S(2)}, u32[]{:S(2)}) collective-permute-start(bf16[400,1408]{1,0:T(8,128)(2,1)S(1)} %pad_maximum_fusion.12), channel_id=1, source_target_pairs={{0,16},{16,0},{1,17},{17,1},{2,18},{18,2},{3,19},{19,3},{4,20},{20... | collective-permute-start | bytes 3379208 | tf_op jit(solution)/shard_map/ppermute | solution.py:44
  138.3 11.8 %collective-permute-start.41 = (bf16[200,1024]{1,0:T(8,128)(2,1)S(1)}, bf16[200,1024]{1,0:T(8,128)(2,1)S(1)}, u32[]{:S(2)}, u32[]{:S(2)}) collective-permute-start(bf16[200,1024]{1,0:T(8,128)(2,1)S(1)} %get-tuple-element.83), channel_id=1, source_target_pairs={{0,3},{1,2},{2,1},{3,0},{4,7},{5,6},{6,5},{7,4},{8,11},{9,10},{10,... | collective-permute-start | bytes 1228808 | tf_op jit(solution)/shard_map/ppermute | solution.py:39
  138.4 20.5 %collective-permute-start.40 = (bf16[200,1024]{1,0:T(8,128)(2,1)S(1)}, bf16[200,1024]{1,0:T(8,128)(2,1)S(1)}, u32[]{:S(2)}, u32[]{:S(2)}) collective-permute-start(bf16[200,1024]{1,0:T(8,128)(2,1)S(1)} %get-tuple-element.84), channel_id=1, source_target_pairs={{0,2},{1,3},{2,0},{3,1},{4,6},{5,7},{6,4},{7,5},{8,10},{9,11},{10,... | collective-permute-start | bytes 1228808 | tf_op jit(solution)/shard_map/ppermute | solution.py:39
  139.8 24.4 %collective-permute-start.39 = (bf16[200,1024]{1,0:T(8,128)(2,1)S(1)}, bf16[200,1024]{1,0:T(8,128)(2,1)S(1)}, u32[]{:S(2)}, u32[]{:S(2)}) collective-permute-start(bf16[200,1024]{1,0:T(8,128)(2,1)S(1)} %get-tuple-element.85), channel_id=1, source_target_pairs={{0,1},{1,0},{2,3},{3,2},{4,5},{5,4},{6,7},{7,6},{8,9},{9,8},{10,11... | collective-permute-start | bytes 1228808 | tf_op jit(solution)/shard_map/ppermute | solution.py:39
  140.2 28.5 %collective-permute-start.21 = (bf16[200,1152]{1,0:T(8,128)(2,1)S(1)}, bf16[200,1152]{1,0:T(8,128)(2,1)S(1)}, u32[]{:S(2)}, u32[]{:S(2)}) collective-permute-start(bf16[200,1152]{1,0:T(8,128)(2,1)S(1)} %get-tuple-element.71), channel_id=1, source_target_pairs={{0,3},{1,2},{2,1},{3,0},{4,7},{5,6},{6,5},{7,4},{8,11},{9,10},{10,... | collective-permute-start | bytes 1382408 | tf_op jit(solution)/shard_map/ppermute | solution.py:39
  150.1 28.5 %collective-permute-start.20 = (bf16[200,1152]{1,0:T(8,128)(2,1)S(1)}, bf16[200,1152]{1,0:T(8,128)(2,1)S(1)}, u32[]{:S(2)}, u32[]{:S(2)}) collective-permute-start(bf16[200,1152]{1,0:T(8,128)(2,1)S(1)} %get-tuple-element.72), channel_id=1, source_target_pairs={{0,2},{1,3},{2,0},{3,1},{4,6},{5,7},{6,4},{7,5},{8,10},{9,11},{10,... | collective-permute-start | bytes 1382408 | tf_op jit(solution)/shard_map/ppermute | solution.py:39
  158.8 19.8 %collective-permute-start.19 = (bf16[200,1152]{1,0:T(8,128)(2,1)S(1)}, bf16[200,1152]{1,0:T(8,128)(2,1)S(1)}, u32[]{:S(2)}, u32[]{:S(2)}) collective-permute-start(bf16[200,1152]{1,0:T(8,128)(2,1)S(1)} %get-tuple-element.73), channel_id=1, source_target_pairs={{0,1},{1,0},{2,3},{3,2},{4,5},{5,4},{6,7},{7,6},{8,9},{9,8},{10,11... | collective-permute-start | bytes 1382408 | tf_op jit(solution)/shard_map/ppermute | solution.py:39
  180.5 40.3 %collective-permute-start.30 = (bf16[400,1408]{1,0:T(8,128)(2,1)S(1)}, bf16[400,1408]{1,0:T(8,128)(2,1)S(1)}, u32[]{:S(2)}, u32[]{:S(2)}) collective-permute-start(bf16[400,1408]{1,0:T(8,128)(2,1)S(1)} %pad_maximum_fusion.13), channel_id=1, source_target_pairs={{0,16},{16,0},{1,17},{17,1},{2,18},{18,2},{3,19},{19,3},{4,20},{20... | collective-permute-start | bytes 3379208 | tf_op jit(solution)/shard_map/ppermute | solution.py:44
  183.7 18.5 %collective-permute-start.27 = (bf16[128,1152]{1,0:T(8,128)(2,1)S(1)}, bf16[128,1152]{1,0:T(8,128)(2,1)S(1)}, u32[]{:S(2)}, u32[]{:S(2)}) collective-permute-start(bf16[128,1152]{1,0:T(8,128)(2,1)S(1)} %get-tuple-element.90), channel_id=1, source_target_pairs={{0,12},{1,13},{2,14},{3,15},{4,0},{5,1},{6,2},{7,3},{8,4},{9,5},{1... | collective-permute-start | bytes 884744 | tf_op jit(solution)/shard_map/ppermute | solution.py:34
  184.0 26.4 %collective-permute-start.29 = (bf16[128,1152]{1,0:T(8,128)(2,1)S(1)}, bf16[128,1152]{1,0:T(8,128)(2,1)S(1)}, u32[]{:S(2)}, u32[]{:S(2)}) collective-permute-start(bf16[128,1152]{1,0:T(8,128)(2,1)S(1)} %get-tuple-element.91), channel_id=1, source_target_pairs={{0,4},{1,5},{2,6},{3,7},{4,8},{5,9},{6,10},{7,11},{8,12},{9,13},{1... | collective-permute-start | bytes 884744 | tf_op jit(solution)/shard_map/ppermute | solution.py:34
  192.7 27.8 %collective-permute-start.28 = (bf16[128,1152]{1,0:T(8,128)(2,1)S(1)}, bf16[128,1152]{1,0:T(8,128)(2,1)S(1)}, u32[]{:S(2)}, u32[]{:S(2)}) collective-permute-start(bf16[128,1152]{1,0:T(8,128)(2,1)S(1)} %get-tuple-element.92), channel_id=1, source_target_pairs={{0,8},{1,9},{2,10},{3,11},{4,12},{5,13},{6,14},{7,15},{8,0},{9,1},... | collective-permute-start | bytes 884744 | tf_op jit(solution)/shard_map/ppermute | solution.py:34
  201.9 18.8 %collective-permute-start.31 = (bf16[200,1024]{1,0:T(8,128)(2,1)S(1)}, bf16[200,1024]{1,0:T(8,128)(2,1)S(1)}, u32[]{:S(2)}, u32[]{:S(2)}) collective-permute-start(bf16[200,1024]{1,0:T(8,128)(2,1)S(1)} %get-tuple-element.98), channel_id=1, source_target_pairs={{0,2},{1,3},{2,0},{3,1},{4,6},{5,7},{6,4},{7,5},{8,10},{9,11},{10,... | collective-permute-start | bytes 1228808 | tf_op jit(solution)/shard_map/ppermute | solution.py:39
  202.2 18.5 %collective-permute-start.32 = (bf16[200,1024]{1,0:T(8,128)(2,1)S(1)}, bf16[200,1024]{1,0:T(8,128)(2,1)S(1)}, u32[]{:S(2)}, u32[]{:S(2)}) collective-permute-start(bf16[200,1024]{1,0:T(8,128)(2,1)S(1)} %get-tuple-element.99), channel_id=1, source_target_pairs={{0,3},{1,2},{2,1},{3,0},{4,7},{5,6},{6,5},{7,4},{8,11},{9,10},{10,... | collective-permute-start | bytes 1228808 | tf_op jit(solution)/shard_map/ppermute | solution.py:39
  223.3 6.0 %collective-permute-start.33 = (bf16[200,1024]{1,0:T(8,128)(2,1)}, bf16[200,1024]{1,0:T(8,128)(2,1)}, u32[]{:S(2)}, u32[]{:S(2)}) collective-permute-start(bf16[200,1024]{1,0:T(8,128)(2,1)} %get-tuple-element.97), channel_id=1, source_target_pairs={{0,1},{1,0},{2,3},{3,2},{4,5},{5,4},{6,7},{7,6},{8,9},{9,8},{10,11... | collective-permute-start | bytes 1228808 | tf_op jit(solution)/shard_map/ppermute | solution.py:39
  226.1 11.4 %collective-permute-start.44 = (bf16[200,1024]{1,0:T(8,128)(2,1)S(1)}, bf16[200,1024]{1,0:T(8,128)(2,1)S(1)}, u32[]{:S(2)}, u32[]{:S(2)}) collective-permute-start(bf16[200,1024]{1,0:T(8,128)(2,1)S(1)} %get-tuple-element.79), channel_id=1, source_target_pairs={{0,3},{1,2},{2,1},{3,0},{4,7},{5,6},{6,5},{7,4},{8,11},{9,10},{10,... | collective-permute-start | bytes 1228808 | tf_op jit(solution)/shard_map/ppermute | solution.py:39
  226.2 20.5 %collective-permute-start.43 = (bf16[200,1024]{1,0:T(8,128)(2,1)S(1)}, bf16[200,1024]{1,0:T(8,128)(2,1)S(1)}, u32[]{:S(2)}, u32[]{:S(2)}) collective-permute-start(bf16[200,1024]{1,0:T(8,128)(2,1)S(1)} %get-tuple-element.80), channel_id=1, source_target_pairs={{0,2},{1,3},{2,0},{3,1},{4,6},{5,7},{6,4},{7,5},{8,10},{9,11},{10,... | collective-permute-start | bytes 1228808 | tf_op jit(solution)/shard_map/ppermute | solution.py:39
  228.1 18.9 %collective-permute-start.42 = (bf16[200,1024]{1,0:T(8,128)(2,1)S(1)}, bf16[200,1024]{1,0:T(8,128)(2,1)S(1)}, u32[]{:S(2)}, u32[]{:S(2)}) collective-permute-start(bf16[200,1024]{1,0:T(8,128)(2,1)S(1)} %get-tuple-element.81), channel_id=1, source_target_pairs={{0,1},{1,0},{2,3},{3,2},{4,5},{5,4},{6,7},{7,6},{8,9},{9,8},{10,11... | collective-permute-start | bytes 1228808 | tf_op jit(solution)/shard_map/ppermute | solution.py:39
  228.1 34.0 %collective-permute-start.37 = (bf16[352,2048]{1,0:T(8,128)(2,1)S(1)}, bf16[352,2048]{1,0:T(8,128)(2,1)S(1)}, u32[]{:S(2)}, u32[]{:S(2)}) collective-permute-start(bf16[352,2048]{1,0:T(8,128)(2,1)S(1)} %copy-done.11), channel_id=1, source_target_pairs={{0,16},{16,0},{1,17},{17,1},{2,18},{18,2},{3,19},{19,3},{4,20},{20... | collective-permute-start | bytes 4325384 | tf_op jit(solution)/shard_map/ppermute | solution.py:44
  231.8 20.7 %collective-permute-start.34 = (bf16[128,1024]{1,0:T(8,128)(2,1)S(1)}, bf16[128,1024]{1,0:T(8,128)(2,1)S(1)}, u32[]{:S(2)}, u32[]{:S(2)}) collective-permute-start(bf16[128,1024]{1,0:T(8,128)(2,1)S(1)} %get-tuple-element.93), channel_id=1, source_target_pairs={{0,12},{1,13},{2,14},{3,15},{4,0},{5,1},{6,2},{7,3},{8,4},{9,5},{1... | collective-permute-start | bytes 786440 | tf_op jit(solution)/shard_map/ppermute | solution.py:34
  237.5 15.0 %collective-permute-start.36 = (bf16[128,1024]{1,0:T(8,128)(2,1)S(1)}, bf16[128,1024]{1,0:T(8,128)(2,1)S(1)}, u32[]{:S(2)}, u32[]{:S(2)}) collective-permute-start(bf16[128,1024]{1,0:T(8,128)(2,1)S(1)} %get-tuple-element.94), channel_id=1, source_target_pairs={{0,4},{1,5},{2,6},{3,7},{4,8},{5,9},{6,10},{7,11},{8,12},{9,13},{1... | collective-permute-start | bytes 786440 | tf_op jit(solution)/shard_map/ppermute | solution.py:34
  246.7 14.4 %collective-permute-start.35 = (bf16[128,1024]{1,0:T(8,128)(2,1)S(1)}, bf16[128,1024]{1,0:T(8,128)(2,1)S(1)}, u32[]{:S(2)}, u32[]{:S(2)}) collective-permute-start(bf16[128,1024]{1,0:T(8,128)(2,1)S(1)} %get-tuple-element.95), channel_id=1, source_target_pairs={{0,8},{1,9},{2,10},{3,11},{4,12},{5,13},{6,14},{7,15},{8,0},{9,1},... | collective-permute-start | bytes 786440 | tf_op jit(solution)/shard_map/ppermute | solution.py:34
  262.1 7.9 %collective-permute-start.38 = (bf16[128,1024]{1,0:T(8,128)(2,1)S(1)}, bf16[128,1024]{1,0:T(8,128)(2,1)S(1)}, u32[]{:S(2)}, u32[]{:S(2)}) collective-permute-start(bf16[128,1024]{1,0:T(8,128)(2,1)S(1)} %convert_add_fusion.1), channel_id=1, source_target_pairs={{0,16},{16,0},{1,17},{17,1},{2,18},{18,2},{3,19},{19,3},{4,20},{20... | collective-permute-start | bytes 786440 | tf_op jit(solution)/shard_map/ppermute | solution.py:44
  (40 other events, 350.1 us)

commit v2 on v1

--- a/solution.py
+++ b/solution.py
@@ -46,8 +46,10 @@
     def part_of(v, index, size, axis):
         return lax.dynamic_slice_in_dim(v, index * size, size, axis)
 
-    def after(v, *others):
-        return lax.optimization_barrier((v, *others))[0]
+    def follow(v, *others):
+        for other in others:
+            v = v + (other[:1, :1].astype(F32) * 0.0).astype(v.dtype)
+        return v
 
     names = jnp.arange(experts, dtype=jnp.int32)
     hits = routes[:, :, None] == names[None, None, :]
@@ -62,7 +64,6 @@
     lane = jnp.arange(lanes, dtype=jnp.int32)
 
     piece = -(-line * capacity // 8) * 8
-    half = plane // 2 * piece
     inner = np.arange(piece)
     inside = inner < line * capacity
     wanted = np.full((piece, line), -1.0, np.float32)
@@ -106,13 +107,12 @@
     reorder = order.reshape(-1)[:, None] == jnp.arange(slot_total, dtype=jnp.int32)[None, :]
     saved_rows = pick(reorder.astype(BF16), saved_preacts[0, 0])
     held_marks = stack(marks_line)
-    own_picker = picker(after(held_marks, saved_rows))
-
-    dy_second = lines(after(out_grad[:, cols:], *dy_first))
-    picked_first = pick(after(own_picker, *dy_first), stack(dy_first))
+    own_picker = picker(held_marks)
+
+    dy_second = lines(follow(out_grad[:, cols:], dy_first[1], dy_first[2]))
+    picked_first = pick(own_picker, stack(dy_first))
     rows_first = exchange(picked_first, everyone)
 
-    down_got, picked_first = lax.optimization_barrier((down_got, picked_first))
     down_full = jnp.zeros((hidden, width), BF16)
     for j in range(groups):
         down_full = lax.dynamic_update_slice_in_dim(
@@ -123,38 +123,30 @@
         over_dp(jnp.concatenate([x_parts[j], marks], axis=1), j) for j in range(1, groups)
     ]
 
-    second_in = jnp.concatenate([stack(dy_second), held_marks], axis=1)
-    picked_second = pick(after(own_picker, picked_first, down_full), second_in)
+    dy_a = stack(rows_first)
+    grad_a = dot(dy_a, down_full[:, :cols], ((1,), (1,)))
+    second_in = jnp.concatenate([stack(dy_second), follow(held_marks, grad_a, *x_others)], axis=1)
+    picked_second = pick(own_picker, second_in)
     rows_second = exchange(picked_second, everyone)
-    x_own_line = lines(after(x_parts[0], *dy_second))
-
-    dy_a = stack(rows_first)
-    grad_a = dot(after(dy_a, picked_second), down_full[:, :cols], ((1,), (1,)))
-    x_others_line = [lines(after(v, grad_a)) for v in x_others]
+    x_own_line = lines(follow(x_parts[0], rows_second[1]))
+
     rows_second = stack(rows_second)
     dy_b = rows_second[:, :cols]
     own_lane = (lane == experts + me).astype(F32)
     g_rows = jnp.sum(rows_second[:, cols:].astype(F32) * own_lane, axis=1, keepdims=True)
 
-    def activation(at, previous):
-        saved = after(saved_rows, *previous)[at]
-        gate_pre = saved[:, :hidden].astype(F32)
-        up_pre = saved[:, hidden:].astype(F32)
-        sigmoid_gate = jax.nn.sigmoid(gate_pre)
-        act = (gate_pre * sigmoid_gate * up_pre).astype(BF16)
-        act_grad = grad_a[at] + dot(dy_b[at], down_full[:, cols:], ((1,), (1,)))
-        gate_sums = jnp.sum(act.astype(F32) * act_grad, axis=1, keepdims=True)
-        gate_sums = (gate_sums / jnp.sqrt(F32(width))).astype(BF16)
-        scaled_grad = g_rows[at] * act_grad
-        grad_gate = scaled_grad * up_pre * sigmoid_gate * (1.0 + gate_pre * (1.0 - sigmoid_gate))
-        grad_up = scaled_grad * gate_pre * sigmoid_gate
-        return jnp.concatenate([grad_gate, grad_up], axis=1).astype(BF16), gate_sums, act
-
-    far, far_sums, far_act = activation(slice(half, None), [grad_a])
-    near, near_sums, near_act = activation(slice(0, half), [far])
-
-    far_got = [over_dp(far, j) for j in range(1, groups)]
-    near_got = [over_dp(after(near, *far_got), j) for j in range(1, groups)]
+    gate_pre = saved_rows[:, :hidden].astype(F32)
+    up_pre = saved_rows[:, hidden:].astype(F32)
+    sigmoid_gate = jax.nn.sigmoid(gate_pre)
+    act = (gate_pre * sigmoid_gate * up_pre).astype(BF16)
+    act_grad = grad_a + dot(dy_b, down_full[:, cols:], ((1,), (1,)))
+    gate_sums = jnp.sum(act.astype(F32) * act_grad, axis=1, keepdims=True)
+    gate_sums = (gate_sums / jnp.sqrt(F32(width))).astype(BF16)
+    scaled_grad = g_rows * act_grad
+    grad_gate = scaled_grad * up_pre * sigmoid_gate * (1.0 + gate_pre * (1.0 - sigmoid_gate))
+    grad_up = scaled_grad * gate_pre * sigmoid_gate
+    pre_grad = jnp.concatenate([grad_gate, grad_up], axis=1).astype(BF16)
+    pre_got = [over_dp(pre_grad, j) for j in range(1, groups)]
 
     def back_rows(v):
         return dot(v, gate_up[0], ((1,), (1,))).astype(BF16)
@@ -163,59 +155,50 @@
         dense = dot(p, back, ((0,), (0,))).astype(BF16)
         return [dense[k * tok_rows : (k + 1) * tok_rows] for k in range(line)]
 
+    def moved(values):
+        return [along_line(values[k], -k) for k in range(line)]
+
     def total(values):
         result = values[0].astype(F32)
-        for k in range(1, line):
-            result = result + along_line(values[k], -k).astype(F32)
+        for v in values[1:]:
+            result = result + v.astype(F32)
         return result
 
-    x_own_line, _ = lax.optimization_barrier((x_own_line, near))
-    x_own_picked = pick(own_picker, stack(x_own_line))
-    x_own = exchange(x_own_picked, everyone)
     expert_lane = (lane == me).astype(F32)
-    own_back = stack([back_rows(after(near, x_own_picked)), back_rows(after(far, x_own_picked))])
-    own_sums = stack([near_sums, far_sums]).astype(F32) * expert_lane
-    own_back = jnp.concatenate([own_back, own_sums.astype(BF16)], axis=1)
-    own_back_got = exchange(own_back, everyone)
-
-    act_late = after(stack([near_act, far_act]), own_back)
-    scaled_dy = [(g_rows * v.astype(F32)).astype(BF16) for v in (dy_a, dy_b)]
-    grad_dn_full = jnp.concatenate([dot(act_late, v, ((0,), (0,))) for v in scaled_dy], axis=1)
-
-    x_pickers, x_picked = [], []
-    for j in range(1, groups):
-        held = stack(x_others_line[j - 1])
-        x_pickers.append(picker(after(held[:, part:], grad_dn_full)))
-        x_picked.append(pick(x_pickers[-1], held[:, :part]))
-    far_back = []
-    for v in far_got:
-        far_rows = back_rows(after(v, *x_picked))
-        far_back += [[in_plane(block(far_rows, k - plane // 2), k) for k in everyone if 2 * k >= plane]]
-    own_dense = combine(own_picker, after(stack(own_back_got), far_rows))
-    own_total = total(own_dense)
-    x_other = [exchange(after(v, *far_back[-1]), everyone) for v in x_picked]
+    own_sums = (gate_sums.astype(F32) * expert_lane).astype(BF16)
+    own_back = jnp.concatenate([back_rows(pre_grad), own_sums], axis=1)
+    x_others_line = [lines(follow(v, own_back)) for v in x_others]
+    own_moved = moved(combine(own_picker, stack(exchange(own_back, everyone))))
+    x_own = exchange(pick(own_picker, stack(x_own_line)), everyone)
+
+    g_later = follow(g_rows, pre_grad)
+    scaled_dy = [(g_later * v.astype(F32)).astype(BF16) for v in (dy_a, dy_b)]
+    grad_dn_full = jnp.concatenate([dot(act, v, ((0,), (0,))) for v in scaled_dy], axis=1)
 
     sent = [
         part_of(grad_dn_full, (replica + j) % groups, hidden_part, 0).astype(BF16)
         for j in range(1, groups)
     ]
-    sent = [over_dp(after(sent[j - 1], *near_got), j) for j in range(1, groups)]
-    others = []
-    for j in range(1, groups):
-        near_rows = back_rows(after(near_got[j - 1], *far_back[-1], own_dense[0]))
-        near_back = [in_plane(block(near_rows, k), k) for k in everyone if 2 * k < plane]
-        others.append(combine(x_pickers[j - 1], stack(near_back + far_back[j - 1])))
+    sent = [over_dp(follow(v, pre_got[-1]), j + 1) for j, v in enumerate(sent)]
+    x_other, others = [], []
+    for v, lined in zip(pre_got, x_others_line):
+        held = stack(lined)
+        x_picker = picker(held[:, part:])
+        back = stack(exchange(back_rows(v), everyone))
+        others.append(combine(x_picker, follow(back, *sent, *own_moved[1:])))
+        x_picked = follow(pick(x_picker, held[:, :part]), others[-1][0])
+        x_other.append(exchange(x_picked, everyone))
+    own_total = total(own_moved)
 
     grad_scale = 1.0 / jnp.sqrt(F32(groups * tok_rows * top))
-    whole = [stack([near, far])] + [stack([a, b]) for a, b in zip(near_got, far_got)]
-    x_all = [stack(x_own)] + [stack(v) for v in x_other]
-    x_all[0] = after(x_all[0], others[-1][0])
+    whole = pre_got + [pre_grad]
+    x_all = [stack(v) for v in x_other] + [follow(stack(x_own), *sent)]
     grad_gu = 0.0
     for x_rows, grads in zip(x_all, whole):
         grad_gu = grad_gu + dot(x_rows, grads, ((0,), (0,)))
     grad_gu = grad_gu * grad_scale
 
-    totals = [after(total(v), *sent) for v in others]
+    totals = [total(moved(v)) for v in others]
     others = [over_dp(v.astype(BF16), groups - 1 - j) for j, v in enumerate(totals)]
     grad_dn = part_of(grad_dn_full, replica, hidden_part, 0)
     for v in sent:

time: 272 us -> 249 us (0.915)
  waiting for transfers between devices: 126 us -> 90.5 us
  between operations: 1.55 us -> 9.92 us
  local copies, waits for them, and re-layouts: 17.8 us -> 23.8 us
  starting transfers between devices: 55.9 us -> 52.9 us
    ppermute x21, waiting for transfers between devices: 77.1 us -> 49.7 us  [along_line(): lax.ppermute(v, 'expert', [(i, (i + k * plane) % experts) for i in range(...]
    ppermute x18, waiting for transfers between devices: 43.1 us -> 29.5 us  [in_plane(): return lax.ppermute(v, 'expert', [(i, i ^ k) for i in range(experts)])]
    slice x3 -> x14, local copies, waits for them, and re-layouts: 1.86 us -> 11.1 us  [the longest x13 10.2 us: follow(): v = v + (other[:1, :1].astype(F32) * 0.0).astype(v.dtype)]
    ppermute x6 -> x5, waiting for transfers between devices: 5.67 us -> 11.3 us  [over_dp(): return lax.ppermute(v, 'dp', [(i, (i + j) % groups) for i in range(groups)])]
    add x2 -> x8, other arithmetic: 0.31 us -> 3.41 us  [the longest x6 3.27 us: follow(): v = v + (other[:1, :1].astype(F32) * 0.0).astype(v.dtype)]
    unnamed x89 -> x78, local copies, waits for them, and re-layouts: 4.84 us -> 1.77 us
    ppermute x6 -> x5, starting transfers between devices: 7.54 us -> 4.66 us  [over_dp(): return lax.ppermute(v, 'dp', [(i, (i + j) % groups) for i in range(groups)])]
    dot_general x21 -> x18, matrix products: 53.2 us -> 53.2 us  [dot(): lax.dot_general(a, b, (contract, ((), ())), preferred_element_type=F32)]
  transfers between devices with their start and end apart: 45 -> 44, of which waited for: 18 -> 13; matrix products, arithmetic and copies ran while one was open for 27% -> 35% of each run, Pallas kernels for 0% -> 0%
where the time goes in v2:
time: 249 us; the launch traced here: 248 us
  waiting for transfers between devices  90.5 us (36%)
  matrix products  53.2 us (21%)
  starting transfers between devices  52.9 us (21%)
  local copies, waits for them, and re-layouts  23.8 us (10%)
  other arithmetic  17.4 us (7%)
  between operations  9.92 us (4%)
    dot_general x18, matrix products, dot(): lax.dot_general(a, b, (contract, ((), ())), preferred_element_type=F32)  53.2 us
    ppermute x21, waiting for transfers between devices, along_line(): lax.ppermute(v, 'expert', [(i, (i + k * plane) % experts) for i in range(...  49.7 us
    ppermute x21, starting transfers between devices, along_line(): lax.ppermute(v, 'expert', [(i, (i + k * plane) % experts) for i in range(...  37.1 us
    ppermute x18, waiting for transfers between devices, in_plane(): return lax.ppermute(v, 'expert', [(i, i ^ k) for i in range(experts)])  29.5 us
    ppermute x5, waiting for transfers between devices, over_dp(): return lax.ppermute(v, 'dp', [(i, (i + j) % groups) for i in range(groups)])  11.3 us
    ppermute x18, starting transfers between devices, in_plane(): return lax.ppermute(v, 'expert', [(i, i ^ k) for i in range(experts)])  11.1 us
    slice x13, local copies, waits for them, and re-layouts, follow(): v = v + (other[:1, :1].astype(F32) * 0.0).astype(v.dtype)  10.2 us
  transfers between devices with their start and end apart: 44, of which 13 were waited for; matrix products, arithmetic and copies ran while one was open for 35% of the time, Pallas kernels for 0%

profile of v2, /device:TPU:0, one launch (start us, length us, event | category | flops | bytes accessed | tf_op | source)
XLA Modules:
  0.0 247.8 jit_solution(10240849398836689310)
XLA Ops:
  3.8 5.1 %collective-permute-start.2 = (bf16[128,128]{0,1:T(8,128)(2,1)S(1)}, bf16[128,128]{0,1:T(8,128)(2,1)S(1)}, u32[]{:S(2)}, u32[]{:S(2)}) collective-permute-start(bf16[128,128]{0,1:T(8,128)(2,1)S(1)} %fusion.134), channel_id=1, source_target_pairs={{0,12},{1,13},{2,14},{3,15},{4,0},{5,1},{6,2},{7,3},{8,4},{9,5},{1... | collective-permute-start | bytes 98312 | tf_op jit(solution)/shard_map/ppermute | solution.py:34
  10.9 2.9 %collective-permute-start.8 = (bf16[128,1024]{1,0:T(8,128)(2,1)S(1)}, bf16[128,1024]{1,0:T(8,128)(2,1)}, u32[]{:S(2)}, u32[]{:S(2)}) collective-permute-start(bf16[128,1024]{1,0:T(8,128)(2,1)S(1)} %slice.176), channel_id=1, source_target_pairs={{0,12},{1,13},{2,14},{3,15},{4,0},{5,1},{6,2},{7,3},{8,4},{9,5},{1... | collective-permute-start | bytes 786440 | tf_op jit(solution)/shard_map/ppermute | solution.py:34
  13.8 1.5 collective-permute-start.12
  18.0 1.9 broadcast_in_dim.68
  24.4 15.8 %collective-permute-done.4 = bf16[128,1024]{1,0:T(8,128)(2,1)} collective-permute-done((bf16[128,1024]{1,0:T(8,128)(2,1)S(1)}, bf16[128,1024]{1,0:T(8,128)(2,1)}, u32[]{:S(2)}, u32[]{:S(2)}) %collective-permute-start.4) | collective-permute-done | bytes 262176 | tf_op jit(solution)/shard_map/ppermute | solution.py:34
  40.2 2.1 convolution_convert_fusion.5
  48.9 4.0 %collective-permute-done.13 = bf16[128,1152]{1,0:T(8,128)(2,1)} collective-permute-done((bf16[128,1152]{1,0:T(8,128)(2,1)}, bf16[128,1152]{1,0:T(8,128)(2,1)}, u32[]{:S(2)}, u32[]{:S(2)}) %collective-permute-start.13) | collective-permute-done | bytes 294944 | tf_op jit(solution)/shard_map/ppermute | solution.py:44
  56.0 2.6 %constant_dynamic-update-slice_fusion.1 = bf16[704,2048]{1,0:T(8,128)(2,1)} fusion(bf16[704,2048]{1,0:T(8,128)(2,1)} %constant_dynamic-update-slice_fusion.2, bf16[352,2048]{1,0:T(8,128)(2,1)} %collective-permute-done.12, s32[]{:T(128)S(6)} %select_n.87), kind=kLoop, calls=%fused_computation.187 | loop fusion | bytes 2883588 | tf_op jit(solution)/shard_map/dynamic_update_slice | solution.py:118
  58.6 1.7 collective-permute-start.5
  60.3 6.5 %collective-permute-done.10 = bf16[200,1024]{1,0:T(8,128)(2,1)S(1)} collective-permute-done((bf16[200,1024]{1,0:T(8,128)(2,1)S(1)}, bf16[200,1024]{1,0:T(8,128)(2,1)S(1)}, u32[]{:S(2)}, u32[]{:S(2)}) %collective-permute-start.10) | collective-permute-done | bytes 409632 | tf_op jit(solution)/shard_map/ppermute | solution.py:39
  66.8 3.1 %fusion.76 = f32[800,704]{1,0:T(8,128)S(1)} fusion(bf16[704,2048]{1,0:T(8,128)(2,1)} %constant_dynamic-update-slice_fusion.1, bf16[200,1024]{1,0:T(8,128)(2,1)S(1)} %collective-permute-done.11, bf16[200,1024]{1,0:T(8,128)(2,1)S(1)} %collective-permute-done.10, bf16[200,1024]{1,0:T(8,128)(2,1)S(1)} %collective-permute-done.9, ...), kind=kOutput, calls=%fused_computation.102 | convolution fusion | flops 1159987200 | bytes 5332992 | tf_op jit(solution)/shard_map/dot_general | solution.py:12
  72.3 3.3 %collective-permute-done.6 = bf16[128,1024]{1,0:T(8,128)(2,1)} collective-permute-done((bf16[128,1024]{1,0:T(8,128)(2,1)}, bf16[128,1024]{1,0:T(8,128)(2,1)}, u32[]{:S(2)}, u32[]{:S(2)}) %collective-permute-start.6) | collective-permute-done | bytes 262176 | tf_op jit(solution)/shard_map/ppermute | solution.py:34
  75.6 2.6 %convolution_convert_fusion = bf16[800,1152]{1,0:T(8,128)(2,1)S(1)} fusion(bf16[512,128]{1,0:T(8,128)(2,1)} %copy.21, bf16[128,1024]{1,0:T(8,128)(2,1)} %collective-permute-done.7, bf16[128,1024]{1,0:T(8,128)(2,1)} %collective-permute-done.6, bf16[128,1024]{1,0:T(8,128)(2,1)} %collective-permute-done.5, bf16[128,1024]{1,0:T(8,128)(2,1)} %add_add_fusion, ...), kind=kOutput, calls=%fused_computation.9 | convolution fusion | flops 950538240 | bytes 3432448 | tf_op jit(solution)/shard_map/dot_general | solution.py:12
  78.5 1.6 collective-permute-start.15
  80.3 3.1 %convolution_convert_fusion.1 = bf16[800,1408]{1,0:T(8,128)(2,1)S(1)} fusion(bf16[1,1,784,1408]{3,2,1,0:T(8,128)(2,1)S(1)} %copy-done.30, s32[800]{0:T(1024)S(1)} %select_n.92), kind=kOutput, calls=%fused_computation.10 | convolution fusion | flops 1767948800 | bytes 4463744 | tf_op jit(solution)/shard_map/dot_general | solution.py:12
  84.7 2.3 collective-permute-start.39
  87.0 1.9 collective-permute-start.38
  88.9 2.3 collective-permute-done.16
  91.3 9.9 %collective-permute-done.15 = bf16[200,1152]{1,0:T(8,128)(2,1)S(1)} collective-permute-done((bf16[200,1152]{1,0:T(8,128)(2,1)S(1)}, bf16[200,1152]{1,0:T(8,128)(2,1)S(1)}, u32[]{:S(2)}, u32[]{:S(2)}) %collective-permute-start.15) | collective-permute-done | bytes 460832 | tf_op jit(solution)/shard_map/ppermute | solution.py:39
  101.4 4.1 %fusion.12 = (bf16[800,704]{1,0:T(8,128)(2,1)S(1)}, bf16[800,704]{1,0:T(8,128)(2,1)S(1)}, f32[800]{0:T(1024)S(1)}) fusion(f32[800]{0:T(1024)S(1)} %multiply_reduce_fusion.1, bf16[800,1408]{1,0:T(8,128)(2,1)S(1)} %convolution_convert_fusion.1, f32[800,704]{1,0:T(8,128)S(1)} %copy-done.38, bf16[704,2048]{1,0:T(8,128)(2,1)} %constant_dynamic-update-slice_fusion.1, ...), kind=kOutput, calls=%fused_computation.32 | convolution fusion | flops 1172940032 | bytes 10049792 | tf_op jit(solution)/shard_map/dot_general | solution.py:12
  106.7 2.1 pad_maximum_fusion
  108.8 1.5 collective-permute-start.26
  110.3 4.4 %fusion.28 = bf16[800,1024]{1,0:T(8,128)(2,1)S(1)} fusion(bf16[800,1408]{1,0:T(8,128)(2,1)} %pad_maximum_fusion, bf16[1,1024,1408]{2,1,0:T(8,128)(2,1)S(1)} %copy-done), kind=kOutput, calls=%fused_computation.50 | convolution fusion | flops 2307686400 | bytes 6774784 | tf_op jit(solution)/shard_map/dot_general | solution.py:12
  117.2 3.8 %fusion.35 = f32[704,1024]{1,0:T(8,128)} fusion(f32[800]{0:T(1024)S(1)} %broadcast_add_fusion.1, bf16[200,1152]{1,0:T(8,128)(2,1)S(1)} %collective-permute-done.16, bf16[200,1152]{1,0:T(8,128)(2,1)S(1)} %collective-permute-done.15, bf16[200,1152]{1,0:T(8,128)(2,1)S(1)} %collective-permute-done.14, bf16[200,1152]{1,0:T(8,128)(2,1)S(1)} %get-tuple-element.11, ...), kind=kOutput, calls=%fused_computation.56 | convolution fusion | flops 1166131200 | bytes 7188480 | tf_op jit(solution)/shard_map/dot_general | solution.py:12
  121.0 3.8 %fusion.34 = f32[704,1024]{1,0:T(8,128)} fusion(f32[800]{0:T(1024)S(1)} %broadcast_add_fusion.1, bf16[200,1024]{1,0:T(8,128)(2,1)S(1)} %copy-done.32, bf16[200,1024]{1,0:T(8,128)(2,1)S(1)} %copy-done.34, bf16[200,1024]{1,0:T(8,128)(2,1)S(1)} %copy-done.36, bf16[200,1024]{1,0:T(8,128)(2,1)S(1)} %get-tuple-element.27, ...), kind=kOutput, calls=%fused_computation.55 | convolution fusion | flops 1166131200 | bytes 6983680 | tf_op jit(solution)/shard_map/dot_general | solution.py:12
  126.0 2.2 collective-permute-start.24
  128.2 2.0 collective-permute-start.23
  131.2 1.2 fusion.158
  132.5 1.6 collective-permute-start.19
  134.1 14.1 %collective-permute-done.24 = bf16[128,1152]{1,0:T(8,128)(2,1)S(1)} collective-permute-done((bf16[128,1152]{1,0:T(8,128)(2,1)S(1)}, bf16[128,1152]{1,0:T(8,128)(2,1)S(1)}, u32[]{:S(2)}, u32[]{:S(2)}) %collective-permute-start.24) | collective-permute-done | bytes 294944 | tf_op jit(solution)/shard_map/ppermute | solution.py:34
  150.0 1.3 broadcast_compare_fusion
  151.3 10.7 %collective-permute-done.18 = bf16[200,1152]{1,0:T(8,128)(2,1)} collective-permute-done((bf16[200,1152]{1,0:T(8,128)(2,1)}, bf16[200,1152]{1,0:T(8,128)(2,1)}, u32[]{:S(2)}, u32[]{:S(2)}) %collective-permute-start.18) | collective-permute-done | bytes 460832 | tf_op jit(solution)/shard_map/ppermute | solution.py:39
  162.0 3.1 %convolution_convert_fusion.2 = bf16[512,1152]{1,0:T(8,128)(2,1)S(1)} fusion(bf16[200,1152]{1,0:T(8,128)(2,1)} %collective-permute-done.19, bf16[200,1152]{1,0:T(8,128)(2,1)} %collective-permute-done.18, bf16[200,1152]{1,0:T(8,128)(2,1)} %collective-permute-done.17, bf16[200,1152]{1,0:T(8,128)(2,1)S(1)} %get-tuple-element.7, ...), kind=kOutput, calls=%fused_computation.18 | convolution fusion | flops 951681024 | bytes 3432448 | tf_op jit(solution)/shard_map/dot_general | solution.py:12
  165.3 2.0 collective-permute-start.22
  169.2 1.4 fusion.74
  171.1 4.4 %fusion.31 = bf16[800,1024]{1,0:T(8,128)(2,1)S(1)} fusion(bf16[800,1408]{1,0:T(8,128)(2,1)} %collective-permute-done.26, bf16[1,1024,1408]{2,1,0:T(8,128)(2,1)S(1)} %copy-done), kind=kOutput, calls=%fused_computation.51 | convolution fusion | flops 2307686400 | bytes 6774784 | tf_op jit(solution)/shard_map/dot_general | solution.py:12
  176.7 1.8 collective-permute-done.22
  179.7 8.3 %collective-permute-done.21 = bf16[128,1152]{1,0:T(8,128)(2,1)S(1)} collective-permute-done((bf16[128,1152]{1,0:T(8,128)(2,1)S(1)}, bf16[128,1152]{1,0:T(8,128)(2,1)S(1)}, u32[]{:S(2)}, u32[]{:S(2)}) %collective-permute-start.21) | collective-permute-done | bytes 294944 | tf_op jit(solution)/shard_map/ppermute | solution.py:34
  192.4 7.3 %collective-permute-done.30 = bf16[352,2048]{1,0:T(8,128)(2,1)} collective-permute-done((bf16[352,2048]{1,0:T(8,128)(2,1)}, bf16[352,2048]{1,0:T(8,128)(2,1)}, u32[]{:S(2)}, u32[]{:S(2)}) %collective-permute-start.30) | collective-permute-done | bytes 1441824 | tf_op jit(solution)/shard_map/ppermute | solution.py:44
  202.9 2.9 %fusion.69 = bf16[512,1024]{1,0:T(8,128)(2,1)S(1)} fusion(bf16[200,1024]{1,0:T(8,128)(2,1)} %collective-permute-done.29, bf16[200,1024]{1,0:T(8,128)(2,1)} %collective-permute-done.28, bf16[200,1024]{1,0:T(8,128)(2,1)} %collective-permute-done.27, bf16[200,1024]{1,0:T(8,128)(2,1)} %get-tuple-element.23, pred[100,8,4,128]{3,2,1,0:T(4,128)(4,1)} %bitcast.70, ...), kind=kOutput, calls=%fused_computation.99 | convolution fusion | flops 852492288 | bytes 3096584 | tf_op jit(solution)/shard_map/dot_general | solution.py:12
  210.6 2.4 collective-permute-start.31
  213.0 1.7 collective-permute-start.33
  214.8 5.4 %fusion.54 = f32[1024,1408]{1,0:T(8,128)S(1)} fusion(bf16[800,1408]{1,0:T(8,128)(2,1)} %pad_maximum_fusion, bf16[200,1024]{1,0:T(8,128)(2,1)} %collective-permute-done.43, bf16[200,1024]{1,0:T(8,128)(2,1)S(1)} %collective-permute-done.42, bf16[200,1024]{1,0:T(8,128)(2,1)S(1)} %collective-permute-done.41, bf16[200,1024]{1,0:T(8,128)(2,1)S(1)} %copy-done.11, ...), kind=kOutput, calls=%fused_computation.80 | convolution fusion | flops 2315059200 | bytes 9658370 | tf_op jit(solution)/shard_map/dot_general | solution.py:12
  220.2 1.7 collective-permute-done.31
  221.8 9.3 %collective-permute-start.32 = (bf16[128,1024]{1,0:T(8,128)(2,1)S(1)}, bf16[128,1024]{1,0:T(8,128)(2,1)S(1)}, u32[]{:S(2)}, u32[]{:S(2)}) collective-permute-start(bf16[128,1024]{1,0:T(8,128)(2,1)S(1)} %get-tuple-element.36), channel_id=1, source_target_pairs={{0,8},{1,9},{2,10},{3,11},{4,12},{5,13},{6,14},{7,15},{8,0},{9,1},... | collective-permute-start | bytes 786440 | tf_op jit(solution)/shard_map/ppermute | solution.py:34
  231.1 3.4 %fusion.3 = f32[1,352,2048]{2,1,0:T(8,128)} fusion(s32[]{:T(128)S(6)} %select_n.97, f32[704,1024]{1,0:T(8,128)S(1)} %copy-done.4, f32[704,1024]{1,0:T(8,128)S(1)} %copy-done.2, bf16[352,2048]{1,0:T(8,128)(2,1)} %collective-permute-done.30), kind=kLoop, calls=%fused_computation.22 | loop fusion | flops 2883584 | bytes 10092548 | tf_op jit(solution)/shard_map/broadcast_in_dim | solution.py:221
  234.6 4.6 %collective-permute-done.32 = bf16[128,1024]{1,0:T(8,128)(2,1)S(1)} collective-permute-done((bf16[128,1024]{1,0:T(8,128)(2,1)S(1)}, bf16[128,1024]{1,0:T(8,128)(2,1)S(1)}, u32[]{:S(2)}, u32[]{:S(2)}) %collective-permute-start.32) | collective-permute-done | bytes 262176 | tf_op jit(solution)/shard_map/ppermute | solution.py:34
  239.9 7.1 %multiply_bitcast_fusion = f32[1,1024,1408]{2,1,0:T(8,128)} fusion(f32[1024,1408]{1,0:T(8,128)S(1)} %fusion.54, bf16[800,1408]{1,0:T(8,128)(2,1)} %collective-permute-done.26, bf16[200,1024]{1,0:T(8,128)(2,1)S(1)} %collective-permute-done.37, bf16[200,1024]{1,0:T(8,128)(2,1)S(1)} %collective-permute-done.36, ...), kind=kOutput, calls=%fused_computation.4 | convolution fusion | flops 2316304384 | bytes 15425536 | tf_op jit(solution)/shard_map/dot_general | solution.py:12
  (199 shorter events, 43.7 us)
Async XLA Ops:
  0.6 109.7 %copy-start = (bf16[1,1024,1408]{2,1,0:T(8,128)(2,1)S(1)}, bf16[1,1024,1408]{2,1,0:T(8,128)(2,1)}, u32[]{:S(2)}) copy-start(bf16[1,1024,1408]{2,1,0:T(8,128)(2,1)} %param.17) | copy-start | bytes 8650756
  3.8 18.0 %collective-permute-start.2 = (bf16[128,128]{0,1:T(8,128)(2,1)S(1)}, bf16[128,128]{0,1:T(8,128)(2,1)S(1)}, u32[]{:S(2)}, u32[]{:S(2)}) collective-permute-start(bf16[128,128]{0,1:T(8,128)(2,1)S(1)} %fusion.134), channel_id=1, source_target_pairs={{0,12},{1,13},{2,14},{3,15},{4,0},{5,1},{6,2},{7,3},{8,4},{9,5},{1... | collective-permute-start | bytes 98312 | tf_op jit(solution)/shard_map/ppermute | solution.py:34
  8.9 14.1 %collective-permute-start.1 = (bf16[128,128]{0,1:T(8,128)(2,1)S(1)}, bf16[128,128]{0,1:T(8,128)(2,1)S(1)}, u32[]{:S(2)}, u32[]{:S(2)}) collective-permute-start(bf16[128,128]{0,1:T(8,128)(2,1)S(1)} %fusion.134), channel_id=1, source_target_pairs={{0,8},{1,9},{2,10},{3,11},{4,12},{5,13},{6,14},{7,15},{8,0},{9,1},... | collective-permute-start | bytes 98312 | tf_op jit(solution)/shard_map/ppermute | solution.py:34
  8.9 14.1 %collective-permute-start = (bf16[128,128]{0,1:T(8,128)(2,1)S(1)}, bf16[128,128]{0,1:T(8,128)(2,1)S(1)}, u32[]{:S(2)}, u32[]{:S(2)}) collective-permute-start(bf16[128,128]{0,1:T(8,128)(2,1)S(1)} %fusion.134), channel_id=1, source_target_pairs={{0,4},{1,5},{2,6},{3,7},{4,8},{5,9},{6,10},{7,11},{8,12},{9,13},{1... | collective-permute-start | bytes 98312 | tf_op jit(solution)/shard_map/ppermute | solution.py:34
  10.9 13.5 %collective-permute-start.8 = (bf16[128,1024]{1,0:T(8,128)(2,1)S(1)}, bf16[128,1024]{1,0:T(8,128)(2,1)}, u32[]{:S(2)}, u32[]{:S(2)}) collective-permute-start(bf16[128,1024]{1,0:T(8,128)(2,1)S(1)} %slice.176), channel_id=1, source_target_pairs={{0,12},{1,13},{2,14},{3,15},{4,0},{5,1},{6,2},{7,3},{8,4},{9,5},{1... | collective-permute-start | bytes 786440 | tf_op jit(solution)/shard_map/ppermute | solution.py:34
  13.8 41.5 %collective-permute-start.12 = (bf16[352,2048]{1,0:T(8,128)(2,1)}, bf16[352,2048]{1,0:T(8,128)(2,1)}, u32[]{:S(2)}, u32[]{:S(2)}) collective-permute-start(bf16[352,2048]{1,0:T(8,128)(2,1)} %bitcast.65), channel_id=1, source_target_pairs={{0,16},{16,0},{1,17},{17,1},{2,18},{18,2},{3,19},{19,3},{4,20},{20... | collective-permute-start | bytes 4325384 | tf_op jit(solution)/shard_map/ppermute | solution.py:44
  21.8 18.4 %collective-permute-start.4 = (bf16[128,1024]{1,0:T(8,128)(2,1)S(1)}, bf16[128,1024]{1,0:T(8,128)(2,1)}, u32[]{:S(2)}, u32[]{:S(2)}) collective-permute-start(bf16[128,1024]{1,0:T(8,128)(2,1)S(1)} %slice.176), channel_id=1, source_target_pairs={{0,8},{1,9},{2,10},{3,11},{4,12},{5,13},{6,14},{7,15},{8,0},{9,1},... | collective-permute-start | bytes 786440 | tf_op jit(solution)/shard_map/ppermute | solution.py:34
  23.0 17.2 %collective-permute-start.3 = (bf16[128,1024]{1,0:T(8,128)(2,1)S(1)}, bf16[128,1024]{1,0:T(8,128)(2,1)}, u32[]{:S(2)}, u32[]{:S(2)}) collective-permute-start(bf16[128,1024]{1,0:T(8,128)(2,1)S(1)} %slice.176), channel_id=1, source_target_pairs={{0,4},{1,5},{2,6},{3,7},{4,8},{5,9},{6,10},{7,11},{8,12},{9,13},{1... | collective-permute-start | bytes 786440 | tf_op jit(solution)/shard_map/ppermute | solution.py:34
  23.0 29.9 %collective-permute-start.13 = (bf16[128,1152]{1,0:T(8,128)(2,1)}, bf16[128,1152]{1,0:T(8,128)(2,1)}, u32[]{:S(2)}, u32[]{:S(2)}) collective-permute-start(bf16[128,1152]{1,0:T(8,128)(2,1)} %pad_maximum_fusion.12), channel_id=1, source_target_pairs={{0,16},{16,0},{1,17},{17,1},{2,18},{18,2},{3,19},{19,3},{4,20},{20... | collective-permute-start | bytes 884744 | tf_op jit(solution)/shard_map/ppermute | solution.py:44
  46.2 12.4 %collective-permute-start.11 = (bf16[200,1024]{1,0:T(8,128)(2,1)S(1)}, bf16[200,1024]{1,0:T(8,128)(2,1)S(1)}, u32[]{:S(2)}, u32[]{:S(2)}) collective-permute-start(bf16[200,1024]{1,0:T(8,128)(2,1)S(1)} %get-tuple-element.28), channel_id=1, source_target_pairs={{0,3},{1,2},{2,1},{3,0},{4,7},{5,6},{6,5},{7,4},{8,11},{9,10},{10,... | collective-permute-start | bytes 1228808 | tf_op jit(solution)/shard_map/ppermute | solution.py:39
  47.4 19.4 %collective-permute-start.10 = (bf16[200,1024]{1,0:T(8,128)(2,1)S(1)}, bf16[200,1024]{1,0:T(8,128)(2,1)S(1)}, u32[]{:S(2)}, u32[]{:S(2)}) collective-permute-start(bf16[200,1024]{1,0:T(8,128)(2,1)S(1)} %get-tuple-element.29), channel_id=1, source_target_pairs={{0,2},{1,3},{2,0},{3,1},{4,6},{5,7},{6,4},{7,5},{8,10},{9,11},{10,... | collective-permute-start | bytes 1228808 | tf_op jit(solution)/shard_map/ppermute | solution.py:39
  47.9 18.9 %collective-permute-start.9 = (bf16[200,1024]{1,0:T(8,128)(2,1)S(1)}, bf16[200,1024]{1,0:T(8,128)(2,1)S(1)}, u32[]{:S(2)}, u32[]{:S(2)}) collective-permute-start(bf16[200,1024]{1,0:T(8,128)(2,1)S(1)} %get-tuple-element.30), channel_id=1, source_target_pairs={{0,1},{1,0},{2,3},{3,2},{4,5},{5,4},{6,7},{7,6},{8,9},{9,8},{10,11... | collective-permute-start | bytes 1228808 | tf_op jit(solution)/shard_map/ppermute | solution.py:39
  52.9 19.4 %collective-permute-start.7 = (bf16[128,1024]{1,0:T(8,128)(2,1)}, bf16[128,1024]{1,0:T(8,128)(2,1)}, u32[]{:S(2)}, u32[]{:S(2)}) collective-permute-start(bf16[128,1024]{1,0:T(8,128)(2,1)} %add_add_fusion), channel_id=1, source_target_pairs={{0,12},{1,13},{2,14},{3,15},{4,0},{5,1},{6,2},{7,3},{8,4},{9,5},{1... | collective-permute-start | bytes 786440 | tf_op jit(solution)/shard_map/ppermute | solution.py:34
  55.3 20.3 %collective-permute-start.6 = (bf16[128,1024]{1,0:T(8,128)(2,1)}, bf16[128,1024]{1,0:T(8,128)(2,1)}, u32[]{:S(2)}, u32[]{:S(2)}) collective-permute-start(bf16[128,1024]{1,0:T(8,128)(2,1)} %add_add_fusion), channel_id=1, source_target_pairs={{0,8},{1,9},{2,10},{3,11},{4,12},{5,13},{6,14},{7,15},{8,0},{9,1},... | collective-permute-start | bytes 786440 | tf_op jit(solution)/shard_map/ppermute | solution.py:34
  58.6 17.0 %collective-permute-start.5 = (bf16[128,1024]{1,0:T(8,128)(2,1)}, bf16[128,1024]{1,0:T(8,128)(2,1)}, u32[]{:S(2)}, u32[]{:S(2)}) collective-permute-start(bf16[128,1024]{1,0:T(8,128)(2,1)} %add_add_fusion), channel_id=1, source_target_pairs={{0,4},{1,5},{2,6},{3,7},{4,8},{5,9},{6,10},{7,11},{8,12},{9,13},{1... | collective-permute-start | bytes 786440 | tf_op jit(solution)/shard_map/ppermute | solution.py:34
  78.4 12.9 %collective-permute-start.16 = (bf16[200,1152]{1,0:T(8,128)(2,1)S(1)}, bf16[200,1152]{1,0:T(8,128)(2,1)S(1)}, u32[]{:S(2)}, u32[]{:S(2)}) collective-permute-start(bf16[200,1152]{1,0:T(8,128)(2,1)S(1)} %get-tuple-element.12), channel_id=1, source_target_pairs={{0,3},{1,2},{2,1},{3,0},{4,7},{5,6},{6,5},{7,4},{8,11},{9,10},{10,... | collective-permute-start | bytes 1382408 | tf_op jit(solution)/shard_map/ppermute | solution.py:39
  78.5 22.7 %collective-permute-start.15 = (bf16[200,1152]{1,0:T(8,128)(2,1)S(1)}, bf16[200,1152]{1,0:T(8,128)(2,1)S(1)}, u32[]{:S(2)}, u32[]{:S(2)}) collective-permute-start(bf16[200,1152]{1,0:T(8,128)(2,1)S(1)} %get-tuple-element.13), channel_id=1, source_target_pairs={{0,2},{1,3},{2,0},{3,1},{4,6},{5,7},{6,4},{7,5},{8,10},{9,11},{10,... | collective-permute-start | bytes 1382408 | tf_op jit(solution)/shard_map/ppermute | solution.py:39
  80.0 21.2 %copy-start.29 = (f32[128]{0:T(128)S(1)}, f32[128]{0:T(128)}, u32[]{:S(2)}) copy-start(f32[128]{0:T(128)} %compare_convert_fusion.1) | copy-start | bytes 1540
  80.0 3.4 %collective-permute-start.14 = (bf16[200,1152]{1,0:T(8,128)(2,1)S(1)}, bf16[200,1152]{1,0:T(8,128)(2,1)S(1)}, u32[]{:S(2)}, u32[]{:S(2)}) collective-permute-start(bf16[200,1152]{1,0:T(8,128)(2,1)S(1)} %get-tuple-element.14), channel_id=1, source_target_pairs={{0,1},{1,0},{2,3},{3,2},{4,5},{5,4},{6,7},{7,6},{8,9},{9,8},{10,11... | collective-permute-start | bytes 1382408 | tf_op jit(solution)/shard_map/ppermute | solution.py:39
  80.3 21.1 %copy-start.38 = (f32[800,704]{1,0:T(8,128)S(1)}, f32[800,704]{1,0:T(8,128)}, u32[]{:S(2)}) copy-start(f32[800,704]{1,0:T(8,128)} %copy-done.37) | copy-start | bytes 6758404
  84.6 41.3 %collective-permute-start.40 = (bf16[128,1024]{1,0:T(8,128)(2,1)S(1)}, bf16[128,1024]{1,0:T(8,128)(2,1)S(1)}, u32[]{:S(2)}, u32[]{:S(2)}) collective-permute-start(bf16[128,1024]{1,0:T(8,128)(2,1)S(1)} %dynamic-slice_add_fusion), channel_id=1, source_target_pairs={{0,12},{1,13},{2,14},{3,15},{4,0},{5,1},{6,2},{7,3},{8,4},{9,5},{1... | collective-permute-start | bytes 786440 | tf_op jit(solution)/shard_map/ppermute | solution.py:34
  84.7 43.4 %collective-permute-start.39 = (bf16[128,1024]{1,0:T(8,128)(2,1)S(1)}, bf16[128,1024]{1,0:T(8,128)(2,1)S(1)}, u32[]{:S(2)}, u32[]{:S(2)}) collective-permute-start(bf16[128,1024]{1,0:T(8,128)(2,1)S(1)} %dynamic-slice_add_fusion), channel_id=1, source_target_pairs={{0,8},{1,9},{2,10},{3,11},{4,12},{5,13},{6,14},{7,15},{8,0},{9,1},... | collective-permute-start | bytes 786440 | tf_op jit(solution)/shard_map/ppermute | solution.py:34
  87.0 43.2 %collective-permute-start.38 = (bf16[128,1024]{1,0:T(8,128)(2,1)S(1)}, bf16[128,1024]{1,0:T(8,128)(2,1)S(1)}, u32[]{:S(2)}, u32[]{:S(2)}) collective-permute-start(bf16[128,1024]{1,0:T(8,128)(2,1)S(1)} %dynamic-slice_add_fusion), channel_id=1, source_target_pairs={{0,4},{1,5},{2,6},{3,7},{4,8},{5,9},{6,10},{7,11},{8,12},{9,13},{1... | collective-permute-start | bytes 786440 | tf_op jit(solution)/shard_map/ppermute | solution.py:34
  108.8 58.5 %collective-permute-start.26 = (bf16[800,1408]{1,0:T(8,128)(2,1)}, bf16[800,1408]{1,0:T(8,128)(2,1)}, u32[]{:S(2)}, u32[]{:S(2)}) collective-permute-start(bf16[800,1408]{1,0:T(8,128)(2,1)} %pad_maximum_fusion), channel_id=1, source_target_pairs={{0,16},{16,0},{1,17},{17,1},{2,18},{18,2},{3,19},{19,3},{4,20},{20... | collective-permute-start | bytes 6758408 | tf_op jit(solution)/shard_map/ppermute | solution.py:44
  116.9 32.2 %copy-start.6 = (bf16[128,1152]{1,0:T(8,128)(2,1)}, bf16[128,1152]{1,0:T(8,128)(2,1)S(1)}, u32[]{:S(2)}) copy-start(bf16[128,1152]{1,0:T(8,128)(2,1)S(1)} %broadcast_add_fusion) | copy-start | bytes 884740
  116.9 15.6 %collective-permute-start.25 = (bf16[128,1152]{1,0:T(8,128)(2,1)S(1)}, bf16[128,1152]{1,0:T(8,128)(2,1)S(1)}, u32[]{:S(2)}, u32[]{:S(2)}) collective-permute-start(bf16[128,1152]{1,0:T(8,128)(2,1)S(1)} %broadcast_add_fusion), channel_id=1, source_target_pairs={{0,12},{1,13},{2,14},{3,15},{4,0},{5,1},{6,2},{7,3},{8,4},{9,5},{1... | collective-permute-start | bytes 884744 | tf_op jit(solution)/shard_map/ppermute | solution.py:34
  126.0 22.2 %collective-permute-start.24 = (bf16[128,1152]{1,0:T(8,128)(2,1)S(1)}, bf16[128,1152]{1,0:T(8,128)(2,1)S(1)}, u32[]{:S(2)}, u32[]{:S(2)}) collective-permute-start(bf16[128,1152]{1,0:T(8,128)(2,1)S(1)} %broadcast_add_fusion), channel_id=1, source_target_pairs={{0,8},{1,9},{2,10},{3,11},{4,12},{5,13},{6,14},{7,15},{8,0},{9,1},... | collective-permute-start | bytes 884744 | tf_op jit(solution)/shard_map/ppermute | solution.py:34
  128.2 20.9 %collective-permute-start.23 = (bf16[128,1152]{1,0:T(8,128)(2,1)S(1)}, bf16[128,1152]{1,0:T(8,128)(2,1)S(1)}, u32[]{:S(2)}, u32[]{:S(2)}) collective-permute-start(bf16[128,1152]{1,0:T(8,128)(2,1)S(1)} %broadcast_add_fusion), channel_id=1, source_target_pairs={{0,4},{1,5},{2,6},{3,7},{4,8},{5,9},{6,10},{7,11},{8,12},{9,13},{1... | collective-permute-start | bytes 884744 | tf_op jit(solution)/shard_map/ppermute | solution.py:34
  130.2 21.2 %collective-permute-start.17 = (bf16[200,1152]{1,0:T(8,128)(2,1)}, bf16[200,1152]{1,0:T(8,128)(2,1)}, u32[]{:S(2)}, u32[]{:S(2)}) collective-permute-start(bf16[200,1152]{1,0:T(8,128)(2,1)} %get-tuple-element.8), channel_id=1, source_target_pairs={{0,1},{1,0},{2,3},{3,2},{4,5},{5,4},{6,7},{7,6},{8,9},{9,8},{10,11... | collective-permute-start | bytes 1382408 | tf_op jit(solution)/shard_map/ppermute | solution.py:39
  132.5 18.9 %collective-permute-start.19 = (bf16[200,1152]{1,0:T(8,128)(2,1)}, bf16[200,1152]{1,0:T(8,128)(2,1)}, u32[]{:S(2)}, u32[]{:S(2)}) collective-permute-start(bf16[200,1152]{1,0:T(8,128)(2,1)} %get-tuple-element.9), channel_id=1, source_target_pairs={{0,3},{1,2},{2,1},{3,0},{4,7},{5,6},{6,5},{7,4},{8,11},{9,10},{10,... | collective-permute-start | bytes 1382408 | tf_op jit(solution)/shard_map/ppermute | solution.py:39
  148.2 13.8 %collective-permute-start.18 = (bf16[200,1152]{1,0:T(8,128)(2,1)}, bf16[200,1152]{1,0:T(8,128)(2,1)}, u32[]{:S(2)}, u32[]{:S(2)}) collective-permute-start(bf16[200,1152]{1,0:T(8,128)(2,1)} %get-tuple-element.10), channel_id=1, source_target_pairs={{0,2},{1,3},{2,0},{3,1},{4,6},{5,7},{6,4},{7,5},{8,10},{9,11},{10,... | collective-permute-start | bytes 1382408 | tf_op jit(solution)/shard_map/ppermute | solution.py:39
  149.1 61.4 %collective-permute-start.43 = (bf16[200,1024]{1,0:T(8,128)(2,1)}, bf16[200,1024]{1,0:T(8,128)(2,1)}, u32[]{:S(2)}, u32[]{:S(2)}) collective-permute-start(bf16[200,1024]{1,0:T(8,128)(2,1)} %get-tuple-element.20), channel_id=1, source_target_pairs={{0,3},{1,2},{2,1},{3,0},{4,7},{5,6},{6,5},{7,4},{8,11},{9,10},{10,... | collective-permute-start | bytes 1228808 | tf_op jit(solution)/shard_map/ppermute | solution.py:39
  165.2 11.5 %collective-permute-start.20 = (bf16[128,1152]{1,0:T(8,128)(2,1)S(1)}, bf16[128,1152]{1,0:T(8,128)(2,1)S(1)}, u32[]{:S(2)}, u32[]{:S(2)}) collective-permute-start(bf16[128,1152]{1,0:T(8,128)(2,1)S(1)} %get-tuple-element.31), channel_id=1, source_target_pairs={{0,12},{1,13},{2,14},{3,15},{4,0},{5,1},{6,2},{7,3},{8,4},{9,5},{1... | collective-permute-start | bytes 884744 | tf_op jit(solution)/shard_map/ppermute | solution.py:34
  165.3 13.3 %collective-permute-start.22 = (bf16[128,1152]{1,0:T(8,128)(2,1)S(1)}, bf16[128,1152]{1,0:T(8,128)(2,1)S(1)}, u32[]{:S(2)}, u32[]{:S(2)}) collective-permute-start(bf16[128,1152]{1,0:T(8,128)(2,1)S(1)} %get-tuple-element.32), channel_id=1, source_target_pairs={{0,4},{1,5},{2,6},{3,7},{4,8},{5,9},{6,10},{7,11},{8,12},{9,13},{1... | collective-permute-start | bytes 884744 | tf_op jit(solution)/shard_map/ppermute | solution.py:34
  167.3 20.7 %collective-permute-start.21 = (bf16[128,1152]{1,0:T(8,128)(2,1)S(1)}, bf16[128,1152]{1,0:T(8,128)(2,1)S(1)}, u32[]{:S(2)}, u32[]{:S(2)}) collective-permute-start(bf16[128,1152]{1,0:T(8,128)(2,1)S(1)} %get-tuple-element.33), channel_id=1, source_target_pairs={{0,8},{1,9},{2,10},{3,11},{4,12},{5,13},{6,14},{7,15},{8,0},{9,1},... | collective-permute-start | bytes 884744 | tf_op jit(solution)/shard_map/ppermute | solution.py:34
  170.6 29.1 %collective-permute-start.30 = (bf16[352,2048]{1,0:T(8,128)(2,1)}, bf16[352,2048]{1,0:T(8,128)(2,1)}, u32[]{:S(2)}, u32[]{:S(2)}) collective-permute-start(bf16[352,2048]{1,0:T(8,128)(2,1)} %fusion.74), channel_id=1, source_target_pairs={{0,16},{16,0},{1,17},{17,1},{2,18},{18,2},{3,19},{19,3},{4,20},{20... | collective-permute-start | bytes 4325384 | tf_op jit(solution)/shard_map/ppermute | solution.py:44
  176.7 26.1 %collective-permute-start.29 = (bf16[200,1024]{1,0:T(8,128)(2,1)}, bf16[200,1024]{1,0:T(8,128)(2,1)}, u32[]{:S(2)}, u32[]{:S(2)}) collective-permute-start(bf16[200,1024]{1,0:T(8,128)(2,1)} %get-tuple-element.24), channel_id=1, source_target_pairs={{0,3},{1,2},{2,1},{3,0},{4,7},{5,6},{6,5},{7,4},{8,11},{9,10},{10,... | collective-permute-start | bytes 1228808 | tf_op jit(solution)/shard_map/ppermute | solution.py:39
  178.5 24.3 %collective-permute-start.28 = (bf16[200,1024]{1,0:T(8,128)(2,1)}, bf16[200,1024]{1,0:T(8,128)(2,1)}, u32[]{:S(2)}, u32[]{:S(2)}) collective-permute-start(bf16[200,1024]{1,0:T(8,128)(2,1)} %get-tuple-element.25), channel_id=1, source_target_pairs={{0,2},{1,3},{2,0},{3,1},{4,6},{5,7},{6,4},{7,5},{8,10},{9,11},{10,... | collective-permute-start | bytes 1228808 | tf_op jit(solution)/shard_map/ppermute | solution.py:39
  188.0 14.9 %collective-permute-start.27 = (bf16[200,1024]{1,0:T(8,128)(2,1)}, bf16[200,1024]{1,0:T(8,128)(2,1)}, u32[]{:S(2)}, u32[]{:S(2)}) collective-permute-start(bf16[200,1024]{1,0:T(8,128)(2,1)} %get-tuple-element.26), channel_id=1, source_target_pairs={{0,1},{1,0},{2,3},{3,2},{4,5},{5,4},{6,7},{7,6},{8,9},{9,8},{10,11... | collective-permute-start | bytes 1228808 | tf_op jit(solution)/shard_map/ppermute | solution.py:39
  199.7 10.9 %collective-permute-start.42 = (bf16[200,1024]{1,0:T(8,128)(2,1)}, bf16[200,1024]{1,0:T(8,128)(2,1)S(1)}, u32[]{:S(2)}, u32[]{:S(2)}) collective-permute-start(bf16[200,1024]{1,0:T(8,128)(2,1)} %get-tuple-element.21), channel_id=1, source_target_pairs={{0,2},{1,3},{2,0},{3,1},{4,6},{5,7},{6,4},{7,5},{8,10},{9,11},{10,... | collective-permute-start | bytes 1228808 | tf_op jit(solution)/shard_map/ppermute | solution.py:39
  202.8 10.2 %collective-permute-start.41 = (bf16[200,1024]{1,0:T(8,128)(2,1)}, bf16[200,1024]{1,0:T(8,128)(2,1)S(1)}, u32[]{:S(2)}, u32[]{:S(2)}) collective-permute-start(bf16[200,1024]{1,0:T(8,128)(2,1)} %get-tuple-element.22), channel_id=1, source_target_pairs={{0,1},{1,0},{2,3},{3,2},{4,5},{5,4},{6,7},{7,6},{8,9},{9,8},{10,11... | collective-permute-start | bytes 1228808 | tf_op jit(solution)/shard_map/ppermute | solution.py:39
  208.3 31.6 %collective-permute-start.37 = (bf16[200,1024]{1,0:T(8,128)(2,1)S(1)}, bf16[200,1024]{1,0:T(8,128)(2,1)S(1)}, u32[]{:S(2)}, u32[]{:S(2)}) collective-permute-start(bf16[200,1024]{1,0:T(8,128)(2,1)S(1)} %get-tuple-element.16), channel_id=1, source_target_pairs={{0,3},{1,2},{2,1},{3,0},{4,7},{5,6},{6,5},{7,4},{8,11},{9,10},{10,... | collective-permute-start | bytes 1228808 | tf_op jit(solution)/shard_map/ppermute | solution.py:39
  209.2 30.7 %collective-permute-start.36 = (bf16[200,1024]{1,0:T(8,128)(2,1)S(1)}, bf16[200,1024]{1,0:T(8,128)(2,1)S(1)}, u32[]{:S(2)}, u32[]{:S(2)}) collective-permute-start(bf16[200,1024]{1,0:T(8,128)(2,1)S(1)} %get-tuple-element.17), channel_id=1, source_target_pairs={{0,2},{1,3},{2,0},{3,1},{4,6},{5,7},{6,4},{7,5},{8,10},{9,11},{10,... | collective-permute-start | bytes 1228808 | tf_op jit(solution)/shard_map/ppermute | solution.py:39
  210.5 29.4 %collective-permute-start.35 = (bf16[200,1024]{1,0:T(8,128)(2,1)S(1)}, bf16[200,1024]{1,0:T(8,128)(2,1)S(1)}, u32[]{:S(2)}, u32[]{:S(2)}) collective-permute-start(bf16[200,1024]{1,0:T(8,128)(2,1)S(1)} %get-tuple-element.18), channel_id=1, source_target_pairs={{0,1},{1,0},{2,3},{3,2},{4,5},{5,4},{6,7},{7,6},{8,9},{9,8},{10,11... | collective-permute-start | bytes 1228808 | tf_op jit(solution)/shard_map/ppermute | solution.py:39
  210.6 11.2 %collective-permute-start.31 = (bf16[128,1024]{1,0:T(8,128)(2,1)S(1)}, bf16[128,1024]{1,0:T(8,128)(2,1)S(1)}, u32[]{:S(2)}, u32[]{:S(2)}) collective-permute-start(bf16[128,1024]{1,0:T(8,128)(2,1)S(1)} %get-tuple-element.34), channel_id=1, source_target_pairs={{0,12},{1,13},{2,14},{3,15},{4,0},{5,1},{6,2},{7,3},{8,4},{9,5},{1... | collective-permute-start | bytes 786440 | tf_op jit(solution)/shard_map/ppermute | solution.py:34
  213.0 21.6 %collective-permute-start.33 = (bf16[128,1024]{1,0:T(8,128)(2,1)S(1)}, bf16[128,1024]{1,0:T(8,128)(2,1)S(1)}, u32[]{:S(2)}, u32[]{:S(2)}) collective-permute-start(bf16[128,1024]{1,0:T(8,128)(2,1)S(1)} %get-tuple-element.35), channel_id=1, source_target_pairs={{0,4},{1,5},{2,6},{3,7},{4,8},{5,9},{6,10},{7,11},{8,12},{9,13},{1... | collective-permute-start | bytes 786440 | tf_op jit(solution)/shard_map/ppermute | solution.py:34
  221.8 17.4 %collective-permute-start.32 = (bf16[128,1024]{1,0:T(8,128)(2,1)S(1)}, bf16[128,1024]{1,0:T(8,128)(2,1)S(1)}, u32[]{:S(2)}, u32[]{:S(2)}) collective-permute-start(bf16[128,1024]{1,0:T(8,128)(2,1)S(1)} %get-tuple-element.36), channel_id=1, source_target_pairs={{0,8},{1,9},{2,10},{3,11},{4,12},{5,13},{6,14},{7,15},{8,0},{9,1},... | collective-permute-start | bytes 786440 | tf_op jit(solution)/shard_map/ppermute | solution.py:34
  239.4 7.6 %collective-permute-start.34 = (bf16[128,1024]{1,0:T(8,128)(2,1)S(1)}, bf16[128,1024]{1,0:T(8,128)(2,1)S(1)}, u32[]{:S(2)}, u32[]{:S(2)}) collective-permute-start(bf16[128,1024]{1,0:T(8,128)(2,1)S(1)} %add_convert_fusion), channel_id=1, source_target_pairs={{0,16},{16,0},{1,17},{17,1},{2,18},{18,2},{3,19},{19,3},{4,20},{20... | collective-permute-start | bytes 786440 | tf_op jit(solution)/shard_map/ppermute | solution.py:44
  (35 other events, 234.0 us)

commit v3 on v2

--- a/solution.py
+++ b/solution.py
@@ -167,8 +167,9 @@
     expert_lane = (lane == me).astype(F32)
     own_sums = (gate_sums.astype(F32) * expert_lane).astype(BF16)
     own_back = jnp.concatenate([back_rows(pre_grad), own_sums], axis=1)
-    x_others_line = [lines(follow(v, own_back)) for v in x_others]
-    own_moved = moved(combine(own_picker, stack(exchange(own_back, everyone))))
+    own_got = exchange(own_back, everyone)
+    x_others_line = [lines(follow(v, own_got[2])) for v in x_others]
+    own_moved = moved(combine(own_picker, stack(own_got)))
     x_own = exchange(pick(own_picker, stack(x_own_line)), everyone)
 
     g_later = follow(g_rows, pre_grad)

time: 249 us -> 270 us (1.084)
  waiting for transfers between devices: 90.5 us -> 128 us
  matrix products: 53.2 us -> 43.2 us
  starting transfers between devices: 52.9 us -> 47.5 us
    ppermute x18, waiting for transfers between devices: 29.5 us -> 47.7 us  [in_plane(): return lax.ppermute(v, 'expert', [(i, i ^ k) for i in range(experts)])]
    ppermute x21, waiting for transfers between devices: 49.7 us -> 67.1 us  [along_line(): lax.ppermute(v, 'expert', [(i, (i + k * plane) % experts) for i in range(...]
    dot_general x18, matrix products: 53.2 us -> 43.2 us  [dot(): lax.dot_general(a, b, (contract, ((), ())), preferred_element_type=F32)]
    ppermute x21, starting transfers between devices: 37.1 us -> 31.7 us  [along_line(): lax.ppermute(v, 'expert', [(i, (i + k * plane) % experts) for i in range(...]
  transfers between devices with their start and end apart: 44 -> 44, of which waited for: 13 -> 18; matrix products, arithmetic and copies ran while one was open for 35% -> 27% of each run, Pallas kernels for 0% -> 0%
where the time goes in v3:
time: 270 us; the launch traced here: 269 us
  waiting for transfers between devices  128 us (47%)
  starting transfers between devices  47.5 us (18%)
  matrix products  43.2 us (16%)
  local copies, waits for them, and re-layouts  25.1 us (9%)
  other arithmetic  15 us (6%)
  between operations  10.1 us (4%)
    ppermute x21, waiting for transfers between devices, along_line(): lax.ppermute(v, 'expert', [(i, (i + k * plane) % experts) for i in range(...  67.1 us
    ppermute x18, waiting for transfers between devices, in_plane(): return lax.ppermute(v, 'expert', [(i, i ^ k) for i in range(experts)])  47.7 us
    dot_general x18, matrix products, dot(): lax.dot_general(a, b, (contract, ((), ())), preferred_element_type=F32)  43.2 us
    ppermute x21, starting transfers between devices, along_line(): lax.ppermute(v, 'expert', [(i, (i + k * plane) % experts) for i in range(...  31.7 us
    ppermute x5, waiting for transfers between devices, over_dp(): return lax.ppermute(v, 'dp', [(i, (i + j) % groups) for i in range(groups)])  13.6 us
    ppermute x18, starting transfers between devices, in_plane(): return lax.ppermute(v, 'expert', [(i, i ^ k) for i in range(experts)])  11 us
    slice x13, local copies, waits for them, and re-layouts, follow(): v = v + (other[:1, :1].astype(F32) * 0.0).astype(v.dtype)  10.9 us
  transfers between devices with their start and end apart: 44, of which 18 were waited for; matrix products, arithmetic and copies ran while one was open for 27% of the time, Pallas kernels for 0%

profile of v3, /device:TPU:0, one launch (start us, length us, event | category | flops | bytes accessed | tf_op | source)
XLA Modules:
  0.0 269.3 jit_solution(6901683597429384872)
XLA Ops:
  3.8 5.1 %collective-permute-start.2 = (bf16[128,128]{0,1:T(8,128)(2,1)S(1)}, bf16[128,128]{0,1:T(8,128)(2,1)S(1)}, u32[]{:S(2)}, u32[]{:S(2)}) collective-permute-start(bf16[128,128]{0,1:T(8,128)(2,1)S(1)} %fusion.134), channel_id=1, source_target_pairs={{0,12},{1,13},{2,14},{3,15},{4,0},{5,1},{6,2},{7,3},{8,4},{9,5},{1... | collective-permute-start | bytes 98312 | tf_op jit(solution)/shard_map/ppermute | solution.py:34
  10.9 2.9 %collective-permute-start.8 = (bf16[128,1024]{1,0:T(8,128)(2,1)S(1)}, bf16[128,1024]{1,0:T(8,128)(2,1)}, u32[]{:S(2)}, u32[]{:S(2)}) collective-permute-start(bf16[128,1024]{1,0:T(8,128)(2,1)S(1)} %slice.176), channel_id=1, source_target_pairs={{0,12},{1,13},{2,14},{3,15},{4,0},{5,1},{6,2},{7,3},{8,4},{9,5},{1... | collective-permute-start | bytes 786440 | tf_op jit(solution)/shard_map/ppermute | solution.py:34
  13.8 1.5 collective-permute-start.12
  18.6 1.9 broadcast_in_dim.68
  25.6 15.9 %collective-permute-done.4 = bf16[128,1024]{1,0:T(8,128)(2,1)} collective-permute-done((bf16[128,1024]{1,0:T(8,128)(2,1)S(1)}, bf16[128,1024]{1,0:T(8,128)(2,1)}, u32[]{:S(2)}, u32[]{:S(2)}) %collective-permute-start.4) | collective-permute-done | bytes 262176 | tf_op jit(solution)/shard_map/ppermute | solution.py:34
  41.4 2.1 convolution_convert_fusion.5
  50.0 2.8 %collective-permute-done.13 = bf16[128,1152]{1,0:T(8,128)(2,1)} collective-permute-done((bf16[128,1152]{1,0:T(8,128)(2,1)}, bf16[128,1152]{1,0:T(8,128)(2,1)}, u32[]{:S(2)}, u32[]{:S(2)}) %collective-permute-start.13) | collective-permute-done | bytes 294944 | tf_op jit(solution)/shard_map/ppermute | solution.py:44
  56.0 2.6 constant_dynamic-update-slice_fusion.1
  59.0 1.3 collective-permute-start.5
  60.3 7.7 %collective-permute-done.10 = bf16[200,1024]{1,0:T(8,128)(2,1)S(1)} collective-permute-done((bf16[200,1024]{1,0:T(8,128)(2,1)S(1)}, bf16[200,1024]{1,0:T(8,128)(2,1)S(1)}, u32[]{:S(2)}, u32[]{:S(2)}) %collective-permute-start.10) | collective-permute-done | bytes 409632 | tf_op jit(solution)/shard_map/ppermute | solution.py:39
  68.0 3.1 %fusion.76 = f32[800,704]{1,0:T(8,128)S(1)} fusion(bf16[704,2048]{1,0:T(8,128)(2,1)} %constant_dynamic-update-slice_fusion.1, bf16[200,1024]{1,0:T(8,128)(2,1)S(1)} %collective-permute-done.11, bf16[200,1024]{1,0:T(8,128)(2,1)S(1)} %collective-permute-done.10, bf16[200,1024]{1,0:T(8,128)(2,1)S(1)} %collective-permute-done.9, ...), kind=kOutput, calls=%fused_computation.102 | convolution fusion | flops 1159987200 | bytes 5332992 | tf_op jit(solution)/shard_map/dot_general | solution.py:12
  72.8 2.8 %collective-permute-done.6 = bf16[128,1024]{1,0:T(8,128)(2,1)} collective-permute-done((bf16[128,1024]{1,0:T(8,128)(2,1)}, bf16[128,1024]{1,0:T(8,128)(2,1)}, u32[]{:S(2)}, u32[]{:S(2)}) %collective-permute-start.6) | collective-permute-done | bytes 262176 | tf_op jit(solution)/shard_map/ppermute | solution.py:34
  75.6 2.5 convolution_convert_fusion
  78.4 1.6 collective-permute-start.15
  80.3 3.1 %convolution_convert_fusion.1 = bf16[800,1408]{1,0:T(8,128)(2,1)S(1)} fusion(bf16[1,1,784,1408]{3,2,1,0:T(8,128)(2,1)S(1)} %copy-done.38, s32[800]{0:T(1024)S(1)} %copy-done.29), kind=kOutput, calls=%fused_computation.10 | convolution fusion | flops 1767948800 | bytes 4463744 | tf_op jit(solution)/shard_map/dot_general | solution.py:12
  84.7 2.3 collective-permute-start.39
  86.9 1.9 collective-permute-start.38
  88.9 2.3 collective-permute-done.16
  91.2 9.9 %collective-permute-done.15 = bf16[200,1152]{1,0:T(8,128)(2,1)S(1)} collective-permute-done((bf16[200,1152]{1,0:T(8,128)(2,1)S(1)}, bf16[200,1152]{1,0:T(8,128)(2,1)S(1)}, u32[]{:S(2)}, u32[]{:S(2)}) %collective-permute-start.15) | collective-permute-done | bytes 460832 | tf_op jit(solution)/shard_map/ppermute | solution.py:39
  101.4 4.1 %fusion.12 = (bf16[800,704]{1,0:T(8,128)(2,1)S(1)}, bf16[800,704]{1,0:T(8,128)(2,1)S(1)}, f32[800]{0:T(1024)S(1)}) fusion(f32[800]{0:T(1024)S(1)} %multiply_reduce_fusion.1, bf16[800,1408]{1,0:T(8,128)(2,1)S(1)} %convolution_convert_fusion.1, f32[800,704]{1,0:T(8,128)S(1)} %copy-done.46, bf16[704,2048]{1,0:T(8,128)(2,1)} %constant_dynamic-update-slice_fusion.1, ...), kind=kOutput, calls=%fused_computation.32 | convolution fusion | flops 1172940032 | bytes 10049792 | tf_op jit(solution)/shard_map/dot_general | solution.py:12
  107.4 1.6 collective-permute-start.26
  109.0 2.7 %fusion.28 = bf16[800,1024]{1,0:T(8,128)(2,1)S(1)} fusion(bf16[800,1408]{1,0:T(8,128)(2,1)S(1)} %pad_maximum_fusion, bf16[1,1024,1408]{2,1,0:T(8,128)(2,1)S(1)} %copy-done), kind=kOutput, calls=%fused_computation.50 | convolution fusion | flops 2307686400 | bytes 6774784 | tf_op jit(solution)/shard_map/dot_general | solution.py:12
  112.2 2.3 fusion.35
  114.5 2.3 fusion.34
  116.9 2.1 collective-permute-start.18
  121.3 19.0 %collective-permute-done.18 = bf16[200,1152]{1,0:T(8,128)(2,1)S(1)} collective-permute-done((bf16[200,1152]{1,0:T(8,128)(2,1)S(1)}, bf16[200,1152]{1,0:T(8,128)(2,1)S(1)}, u32[]{:S(2)}, u32[]{:S(2)}) %collective-permute-start.18) | collective-permute-done | bytes 460832 | tf_op jit(solution)/shard_map/ppermute | solution.py:39
  141.4 1.8 convolution_convert_fusion.2
  143.4 2.0 collective-permute-start.22
  145.4 2.1 collective-permute-start.21
  148.5 9.4 %collective-permute-done.20 = bf16[128,1152]{1,0:T(8,128)(2,1)S(1)} collective-permute-done((bf16[128,1152]{1,0:T(8,128)(2,1)S(1)}, bf16[128,1152]{1,0:T(8,128)(2,1)S(1)}, u32[]{:S(2)}, u32[]{:S(2)}) %collective-permute-start.20) | collective-permute-done | bytes 294944 | tf_op jit(solution)/shard_map/ppermute | solution.py:34
  158.0 3.4 %collective-permute-done.22 = bf16[128,1152]{1,0:T(8,128)(2,1)S(1)} collective-permute-done((bf16[128,1152]{1,0:T(8,128)(2,1)S(1)}, bf16[128,1152]{1,0:T(8,128)(2,1)S(1)}, u32[]{:S(2)}, u32[]{:S(2)}) %collective-permute-start.22) | collective-permute-done | bytes 294944 | tf_op jit(solution)/shard_map/ppermute | solution.py:34
  161.3 5.3 %collective-permute-start.24 = (bf16[128,1152]{1,0:T(8,128)(2,1)S(1)}, bf16[128,1152]{1,0:T(8,128)(2,1)S(1)}, u32[]{:S(2)}, u32[]{:S(2)}) collective-permute-start(bf16[128,1152]{1,0:T(8,128)(2,1)S(1)} %broadcast_add_fusion), channel_id=1, source_target_pairs={{0,8},{1,9},{2,10},{3,11},{4,12},{5,13},{6,14},{7,15},{8,0},{9,1},... | collective-permute-start | bytes 884744 | tf_op jit(solution)/shard_map/ppermute | solution.py:34
  166.6 12.2 %collective-permute-done.21 = bf16[128,1152]{1,0:T(8,128)(2,1)S(1)} collective-permute-done((bf16[128,1152]{1,0:T(8,128)(2,1)S(1)}, bf16[128,1152]{1,0:T(8,128)(2,1)S(1)}, u32[]{:S(2)}, u32[]{:S(2)}) %collective-permute-start.21) | collective-permute-done | bytes 294944 | tf_op jit(solution)/shard_map/ppermute | solution.py:34
  178.8 3.3 %collective-permute-start.23 = (bf16[128,1152]{1,0:T(8,128)(2,1)S(1)}, bf16[128,1152]{1,0:T(8,128)(2,1)S(1)}, u32[]{:S(2)}, u32[]{:S(2)}) collective-permute-start(bf16[128,1152]{1,0:T(8,128)(2,1)S(1)} %broadcast_add_fusion), channel_id=1, source_target_pairs={{0,4},{1,5},{2,6},{3,7},{4,8},{5,9},{6,10},{7,11},{8,12},{9,13},{1... | collective-permute-start | bytes 884744 | tf_op jit(solution)/shard_map/ppermute | solution.py:34
  184.4 1.5 fusion.74
  186.4 9.5 %collective-permute-done.24 = bf16[128,1152]{1,0:T(8,128)(2,1)S(1)} collective-permute-done((bf16[128,1152]{1,0:T(8,128)(2,1)S(1)}, bf16[128,1152]{1,0:T(8,128)(2,1)S(1)}, u32[]{:S(2)}, u32[]{:S(2)}) %collective-permute-start.24) | collective-permute-done | bytes 294944 | tf_op jit(solution)/shard_map/ppermute | solution.py:34
  202.4 4.4 %fusion.31 = bf16[800,1024]{1,0:T(8,128)(2,1)S(1)} fusion(bf16[800,1408]{1,0:T(8,128)(2,1)} %copy-done.36, bf16[1,1024,1408]{2,1,0:T(8,128)(2,1)S(1)} %copy-done), kind=kOutput, calls=%fused_computation.51 | convolution fusion | flops 2307686400 | bytes 6774784 | tf_op jit(solution)/shard_map/dot_general | solution.py:12
  207.1 1.6 collective-permute-start.28
  210.1 9.2 %collective-permute-done.30 = bf16[352,2048]{1,0:T(8,128)(2,1)} collective-permute-done((bf16[352,2048]{1,0:T(8,128)(2,1)}, bf16[352,2048]{1,0:T(8,128)(2,1)}, u32[]{:S(2)}, u32[]{:S(2)}) %collective-permute-start.30) | collective-permute-done | bytes 1441824 | tf_op jit(solution)/shard_map/ppermute | solution.py:44
  222.2 5.5 %collective-permute-done.28 = bf16[200,1024]{1,0:T(8,128)(2,1)S(1)} collective-permute-done((bf16[200,1024]{1,0:T(8,128)(2,1)S(1)}, bf16[200,1024]{1,0:T(8,128)(2,1)S(1)}, u32[]{:S(2)}, u32[]{:S(2)}) %collective-permute-start.28) | collective-permute-done | bytes 409632 | tf_op jit(solution)/shard_map/ppermute | solution.py:39
  227.7 1.4 fusion.69
  233.5 2.9 %collective-permute-done.42 = bf16[200,1024]{1,0:T(8,128)(2,1)S(1)} collective-permute-done((bf16[200,1024]{1,0:T(8,128)(2,1)S(1)}, bf16[200,1024]{1,0:T(8,128)(2,1)S(1)}, u32[]{:S(2)}, u32[]{:S(2)}) %collective-permute-start.42) | collective-permute-done | bytes 409632 | tf_op jit(solution)/shard_map/ppermute | solution.py:39
  238.5 4.6 %fusion.54 = f32[1024,1408]{1,0:T(8,128)S(1)} fusion(bf16[800,1408]{1,0:T(8,128)(2,1)S(1)} %copy-done.6, bf16[200,1024]{1,0:T(8,128)(2,1)} %collective-permute-done.43, bf16[200,1024]{1,0:T(8,128)(2,1)S(1)} %collective-permute-done.42, bf16[200,1024]{1,0:T(8,128)(2,1)S(1)} %collective-permute-done.41, bf16[200,1024]{1,0:T(8,128)(2,1)S(1)} %copy-done.13, ...), kind=kOutput, calls=%fused_computation.80 | convolution fusion | flops 2315059200 | bytes 9658370 | tf_op jit(solution)/shard_map/dot_general | solution.py:12
  243.1 6.5 %collective-permute-done.31 = bf16[128,1024]{1,0:T(8,128)(2,1)S(1)} collective-permute-done((bf16[128,1024]{1,0:T(8,128)(2,1)S(1)}, bf16[128,1024]{1,0:T(8,128)(2,1)S(1)}, u32[]{:S(2)}, u32[]{:S(2)}) %collective-permute-start.31) | collective-permute-done | bytes 262176 | tf_op jit(solution)/shard_map/ppermute | solution.py:34
  249.6 3.5 %fusion.3 = f32[1,352,2048]{2,1,0:T(8,128)} fusion(s32[]{:T(128)S(6)} %select_n.97, f32[704,1024]{1,0:T(8,128)S(1)} %copy-done.4, f32[704,1024]{1,0:T(8,128)S(1)} %copy-done.2, bf16[352,2048]{1,0:T(8,128)(2,1)} %collective-permute-done.30), kind=kLoop, calls=%fused_computation.22 | loop fusion | flops 2883584 | bytes 10092548 | tf_op jit(solution)/shard_map/broadcast_in_dim | solution.py:222
  253.2 7.5 %collective-permute-done.32 = bf16[128,1024]{1,0:T(8,128)(2,1)S(1)} collective-permute-done((bf16[128,1024]{1,0:T(8,128)(2,1)S(1)}, bf16[128,1024]{1,0:T(8,128)(2,1)S(1)}, u32[]{:S(2)}, u32[]{:S(2)}) %collective-permute-start.32) | collective-permute-done | bytes 262176 | tf_op jit(solution)/shard_map/ppermute | solution.py:34
  261.5 5.5 %multiply_bitcast_fusion = f32[1,1024,1408]{2,1,0:T(8,128)} fusion(f32[1024,1408]{1,0:T(8,128)S(1)} %fusion.54, bf16[800,1408]{1,0:T(8,128)(2,1)S(1)} %copy-done.37, bf16[200,1024]{1,0:T(8,128)(2,1)S(1)} %collective-permute-done.37, bf16[200,1024]{1,0:T(8,128)(2,1)S(1)} %collective-permute-done.36, bf16[200,1024]{1,0:T(8,128)(2,1)S(1)} %collective-permute-done.35, ...), kind=kOutput, calls=%fused_computation.4 | convolution fusion | flops 2316304384 | bytes 15425536 | tf_op jit(solution)/shard_map/dot_general | solution.py:12
  266.9 1.5 collective-permute-done.34
  (215 shorter events, 47.2 us)
Async XLA Ops:
  0.6 108.3 %copy-start = (bf16[1,1024,1408]{2,1,0:T(8,128)(2,1)S(1)}, bf16[1,1024,1408]{2,1,0:T(8,128)(2,1)}, u32[]{:S(2)}) copy-start(bf16[1,1024,1408]{2,1,0:T(8,128)(2,1)} %param.17) | copy-start | bytes 8650756
  3.8 19.3 %collective-permute-start.2 = (bf16[128,128]{0,1:T(8,128)(2,1)S(1)}, bf16[128,128]{0,1:T(8,128)(2,1)S(1)}, u32[]{:S(2)}, u32[]{:S(2)}) collective-permute-start(bf16[128,128]{0,1:T(8,128)(2,1)S(1)} %fusion.134), channel_id=1, source_target_pairs={{0,12},{1,13},{2,14},{3,15},{4,0},{5,1},{6,2},{7,3},{8,4},{9,5},{1... | collective-permute-start | bytes 98312 | tf_op jit(solution)/shard_map/ppermute | solution.py:34
  8.9 15.3 %collective-permute-start.1 = (bf16[128,128]{0,1:T(8,128)(2,1)S(1)}, bf16[128,128]{0,1:T(8,128)(2,1)S(1)}, u32[]{:S(2)}, u32[]{:S(2)}) collective-permute-start(bf16[128,128]{0,1:T(8,128)(2,1)S(1)} %fusion.134), channel_id=1, source_target_pairs={{0,8},{1,9},{2,10},{3,11},{4,12},{5,13},{6,14},{7,15},{8,0},{9,1},... | collective-permute-start | bytes 98312 | tf_op jit(solution)/shard_map/ppermute | solution.py:34
  8.9 15.3 %collective-permute-start = (bf16[128,128]{0,1:T(8,128)(2,1)S(1)}, bf16[128,128]{0,1:T(8,128)(2,1)S(1)}, u32[]{:S(2)}, u32[]{:S(2)}) collective-permute-start(bf16[128,128]{0,1:T(8,128)(2,1)S(1)} %fusion.134), channel_id=1, source_target_pairs={{0,4},{1,5},{2,6},{3,7},{4,8},{5,9},{6,10},{7,11},{8,12},{9,13},{1... | collective-permute-start | bytes 98312 | tf_op jit(solution)/shard_map/ppermute | solution.py:34
  10.9 14.6 %collective-permute-start.8 = (bf16[128,1024]{1,0:T(8,128)(2,1)S(1)}, bf16[128,1024]{1,0:T(8,128)(2,1)}, u32[]{:S(2)}, u32[]{:S(2)}) collective-permute-start(bf16[128,1024]{1,0:T(8,128)(2,1)S(1)} %slice.176), channel_id=1, source_target_pairs={{0,12},{1,13},{2,14},{3,15},{4,0},{5,1},{6,2},{7,3},{8,4},{9,5},{1... | collective-permute-start | bytes 786440 | tf_op jit(solution)/shard_map/ppermute | solution.py:34
  13.8 41.5 %collective-permute-start.12 = (bf16[352,2048]{1,0:T(8,128)(2,1)}, bf16[352,2048]{1,0:T(8,128)(2,1)}, u32[]{:S(2)}, u32[]{:S(2)}) collective-permute-start(bf16[352,2048]{1,0:T(8,128)(2,1)} %bitcast.65), channel_id=1, source_target_pairs={{0,16},{16,0},{1,17},{17,1},{2,18},{18,2},{3,19},{19,3},{4,20},{20... | collective-permute-start | bytes 4325384 | tf_op jit(solution)/shard_map/ppermute | solution.py:44
  23.1 18.3 %collective-permute-start.4 = (bf16[128,1024]{1,0:T(8,128)(2,1)S(1)}, bf16[128,1024]{1,0:T(8,128)(2,1)}, u32[]{:S(2)}, u32[]{:S(2)}) collective-permute-start(bf16[128,1024]{1,0:T(8,128)(2,1)S(1)} %slice.176), channel_id=1, source_target_pairs={{0,8},{1,9},{2,10},{3,11},{4,12},{5,13},{6,14},{7,15},{8,0},{9,1},... | collective-permute-start | bytes 786440 | tf_op jit(solution)/shard_map/ppermute | solution.py:34
  24.2 17.2 %collective-permute-start.3 = (bf16[128,1024]{1,0:T(8,128)(2,1)S(1)}, bf16[128,1024]{1,0:T(8,128)(2,1)}, u32[]{:S(2)}, u32[]{:S(2)}) collective-permute-start(bf16[128,1024]{1,0:T(8,128)(2,1)S(1)} %slice.176), channel_id=1, source_target_pairs={{0,4},{1,5},{2,6},{3,7},{4,8},{5,9},{6,10},{7,11},{8,12},{9,13},{1... | collective-permute-start | bytes 786440 | tf_op jit(solution)/shard_map/ppermute | solution.py:34
  24.2 28.7 %collective-permute-start.13 = (bf16[128,1152]{1,0:T(8,128)(2,1)}, bf16[128,1152]{1,0:T(8,128)(2,1)}, u32[]{:S(2)}, u32[]{:S(2)}) collective-permute-start(bf16[128,1152]{1,0:T(8,128)(2,1)} %pad_maximum_fusion.12), channel_id=1, source_target_pairs={{0,16},{16,0},{1,17},{17,1},{2,18},{18,2},{3,19},{19,3},{4,20},{20... | collective-permute-start | bytes 884744 | tf_op jit(solution)/shard_map/ppermute | solution.py:44
  47.4 11.6 %collective-permute-start.11 = (bf16[200,1024]{1,0:T(8,128)(2,1)S(1)}, bf16[200,1024]{1,0:T(8,128)(2,1)S(1)}, u32[]{:S(2)}, u32[]{:S(2)}) collective-permute-start(bf16[200,1024]{1,0:T(8,128)(2,1)S(1)} %get-tuple-element.28), channel_id=1, source_target_pairs={{0,3},{1,2},{2,1},{3,0},{4,7},{5,6},{6,5},{7,4},{8,11},{9,10},{10,... | collective-permute-start | bytes 1228808 | tf_op jit(solution)/shard_map/ppermute | solution.py:39
  48.6 19.4 %collective-permute-start.10 = (bf16[200,1024]{1,0:T(8,128)(2,1)S(1)}, bf16[200,1024]{1,0:T(8,128)(2,1)S(1)}, u32[]{:S(2)}, u32[]{:S(2)}) collective-permute-start(bf16[200,1024]{1,0:T(8,128)(2,1)S(1)} %get-tuple-element.29), channel_id=1, source_target_pairs={{0,2},{1,3},{2,0},{3,1},{4,6},{5,7},{6,4},{7,5},{8,10},{9,11},{10,... | collective-permute-start | bytes 1228808 | tf_op jit(solution)/shard_map/ppermute | solution.py:39
  49.1 18.9 %collective-permute-start.9 = (bf16[200,1024]{1,0:T(8,128)(2,1)S(1)}, bf16[200,1024]{1,0:T(8,128)(2,1)S(1)}, u32[]{:S(2)}, u32[]{:S(2)}) collective-permute-start(bf16[200,1024]{1,0:T(8,128)(2,1)S(1)} %get-tuple-element.30), channel_id=1, source_target_pairs={{0,1},{1,0},{2,3},{3,2},{4,5},{5,4},{6,7},{7,6},{8,9},{9,8},{10,11... | collective-permute-start | bytes 1228808 | tf_op jit(solution)/shard_map/ppermute | solution.py:39
  52.9 19.9 %collective-permute-start.7 = (bf16[128,1024]{1,0:T(8,128)(2,1)}, bf16[128,1024]{1,0:T(8,128)(2,1)}, u32[]{:S(2)}, u32[]{:S(2)}) collective-permute-start(bf16[128,1024]{1,0:T(8,128)(2,1)} %add_add_fusion), channel_id=1, source_target_pairs={{0,12},{1,13},{2,14},{3,15},{4,0},{5,1},{6,2},{7,3},{8,4},{9,5},{1... | collective-permute-start | bytes 786440 | tf_op jit(solution)/shard_map/ppermute | solution.py:34
  55.3 20.3 %collective-permute-start.6 = (bf16[128,1024]{1,0:T(8,128)(2,1)}, bf16[128,1024]{1,0:T(8,128)(2,1)}, u32[]{:S(2)}, u32[]{:S(2)}) collective-permute-start(bf16[128,1024]{1,0:T(8,128)(2,1)} %add_add_fusion), channel_id=1, source_target_pairs={{0,8},{1,9},{2,10},{3,11},{4,12},{5,13},{6,14},{7,15},{8,0},{9,1},... | collective-permute-start | bytes 786440 | tf_op jit(solution)/shard_map/ppermute | solution.py:34
  59.0 16.6 %collective-permute-start.5 = (bf16[128,1024]{1,0:T(8,128)(2,1)}, bf16[128,1024]{1,0:T(8,128)(2,1)}, u32[]{:S(2)}, u32[]{:S(2)}) collective-permute-start(bf16[128,1024]{1,0:T(8,128)(2,1)} %add_add_fusion), channel_id=1, source_target_pairs={{0,4},{1,5},{2,6},{3,7},{4,8},{5,9},{6,10},{7,11},{8,12},{9,13},{1... | collective-permute-start | bytes 786440 | tf_op jit(solution)/shard_map/ppermute | solution.py:34
  78.3 12.9 %collective-permute-start.16 = (bf16[200,1152]{1,0:T(8,128)(2,1)S(1)}, bf16[200,1152]{1,0:T(8,128)(2,1)S(1)}, u32[]{:S(2)}, u32[]{:S(2)}) collective-permute-start(bf16[200,1152]{1,0:T(8,128)(2,1)S(1)} %get-tuple-element.12), channel_id=1, source_target_pairs={{0,3},{1,2},{2,1},{3,0},{4,7},{5,6},{6,5},{7,4},{8,11},{9,10},{10,... | collective-permute-start | bytes 1382408 | tf_op jit(solution)/shard_map/ppermute | solution.py:39
  78.4 22.7 %collective-permute-start.15 = (bf16[200,1152]{1,0:T(8,128)(2,1)S(1)}, bf16[200,1152]{1,0:T(8,128)(2,1)S(1)}, u32[]{:S(2)}, u32[]{:S(2)}) collective-permute-start(bf16[200,1152]{1,0:T(8,128)(2,1)S(1)} %get-tuple-element.13), channel_id=1, source_target_pairs={{0,2},{1,3},{2,0},{3,1},{4,6},{5,7},{6,4},{7,5},{8,10},{9,11},{10,... | collective-permute-start | bytes 1382408 | tf_op jit(solution)/shard_map/ppermute | solution.py:39
  80.0 3.4 %collective-permute-start.14 = (bf16[200,1152]{1,0:T(8,128)(2,1)S(1)}, bf16[200,1152]{1,0:T(8,128)(2,1)S(1)}, u32[]{:S(2)}, u32[]{:S(2)}) collective-permute-start(bf16[200,1152]{1,0:T(8,128)(2,1)S(1)} %get-tuple-element.14), channel_id=1, source_target_pairs={{0,1},{1,0},{2,3},{3,2},{4,5},{5,4},{6,7},{7,6},{8,9},{9,8},{10,11... | collective-permute-start | bytes 1382408 | tf_op jit(solution)/shard_map/ppermute | solution.py:39
  84.6 32.2 %collective-permute-start.40 = (bf16[128,1024]{1,0:T(8,128)(2,1)S(1)}, bf16[128,1024]{1,0:T(8,128)(2,1)S(1)}, u32[]{:S(2)}, u32[]{:S(2)}) collective-permute-start(bf16[128,1024]{1,0:T(8,128)(2,1)S(1)} %dynamic-slice_add_fusion), channel_id=1, source_target_pairs={{0,12},{1,13},{2,14},{3,15},{4,0},{5,1},{6,2},{7,3},{8,4},{9,5},{1... | collective-permute-start | bytes 786440 | tf_op jit(solution)/shard_map/ppermute | solution.py:34
  84.7 32.2 %collective-permute-start.39 = (bf16[128,1024]{1,0:T(8,128)(2,1)S(1)}, bf16[128,1024]{1,0:T(8,128)(2,1)S(1)}, u32[]{:S(2)}, u32[]{:S(2)}) collective-permute-start(bf16[128,1024]{1,0:T(8,128)(2,1)S(1)} %dynamic-slice_add_fusion), channel_id=1, source_target_pairs={{0,8},{1,9},{2,10},{3,11},{4,12},{5,13},{6,14},{7,15},{8,0},{9,1},... | collective-permute-start | bytes 786440 | tf_op jit(solution)/shard_map/ppermute | solution.py:34
  86.9 32.1 %collective-permute-start.38 = (bf16[128,1024]{1,0:T(8,128)(2,1)S(1)}, bf16[128,1024]{1,0:T(8,128)(2,1)S(1)}, u32[]{:S(2)}, u32[]{:S(2)}) collective-permute-start(bf16[128,1024]{1,0:T(8,128)(2,1)S(1)} %dynamic-slice_add_fusion), channel_id=1, source_target_pairs={{0,4},{1,5},{2,6},{3,7},{4,8},{5,9},{6,10},{7,11},{8,12},{9,13},{1... | collective-permute-start | bytes 786440 | tf_op jit(solution)/shard_map/ppermute | solution.py:34
  107.4 75.0 %collective-permute-start.26 = (bf16[800,1408]{1,0:T(8,128)(2,1)S(1)}, bf16[800,1408]{1,0:T(8,128)(2,1)S(1)}, u32[]{:S(2)}, u32[]{:S(2)}) collective-permute-start(bf16[800,1408]{1,0:T(8,128)(2,1)S(1)} %pad_maximum_fusion), channel_id=1, source_target_pairs={{0,16},{16,0},{1,17},{17,1},{2,18},{18,2},{3,19},{19,3},{4,20},{20... | collective-permute-start | bytes 6758408 | tf_op jit(solution)/shard_map/ppermute | solution.py:44
  112.1 29.3 %collective-permute-start.17 = (bf16[200,1152]{1,0:T(8,128)(2,1)S(1)}, bf16[200,1152]{1,0:T(8,128)(2,1)S(1)}, u32[]{:S(2)}, u32[]{:S(2)}) collective-permute-start(bf16[200,1152]{1,0:T(8,128)(2,1)S(1)} %get-tuple-element.8), channel_id=1, source_target_pairs={{0,1},{1,0},{2,3},{3,2},{4,5},{5,4},{6,7},{7,6},{8,9},{9,8},{10,11... | collective-permute-start | bytes 1382408 | tf_op jit(solution)/shard_map/ppermute | solution.py:39
  114.5 69.9 %copy-start.1 = (f32[704,1024]{1,0:T(8,128)}, f32[704,1024]{1,0:T(8,128)S(1)}, u32[]{:S(2)}) copy-start(f32[704,1024]{1,0:T(8,128)S(1)} %fusion.35) | copy-start | bytes 8650756
  116.8 67.6 %copy-start.3 = (f32[704,1024]{1,0:T(8,128)}, f32[704,1024]{1,0:T(8,128)S(1)}, u32[]{:S(2)}) copy-start(f32[704,1024]{1,0:T(8,128)S(1)} %fusion.34) | copy-start | bytes 8650756
  116.8 24.6 %collective-permute-start.19 = (bf16[200,1152]{1,0:T(8,128)(2,1)S(1)}, bf16[200,1152]{1,0:T(8,128)(2,1)S(1)}, u32[]{:S(2)}, u32[]{:S(2)}) collective-permute-start(bf16[200,1152]{1,0:T(8,128)(2,1)S(1)} %get-tuple-element.9), channel_id=1, source_target_pairs={{0,3},{1,2},{2,1},{3,0},{4,7},{5,6},{6,5},{7,4},{8,11},{9,10},{10,... | collective-permute-start | bytes 1382408 | tf_op jit(solution)/shard_map/ppermute | solution.py:39
  116.9 23.4 %collective-permute-start.18 = (bf16[200,1152]{1,0:T(8,128)(2,1)S(1)}, bf16[200,1152]{1,0:T(8,128)(2,1)S(1)}, u32[]{:S(2)}, u32[]{:S(2)}) collective-permute-start(bf16[200,1152]{1,0:T(8,128)(2,1)S(1)} %get-tuple-element.10), channel_id=1, source_target_pairs={{0,2},{1,3},{2,0},{3,1},{4,6},{5,7},{6,4},{7,5},{8,10},{9,11},{10,... | collective-permute-start | bytes 1382408 | tf_op jit(solution)/shard_map/ppermute | solution.py:39
  121.3 112.0 %collective-permute-start.43 = (bf16[200,1024]{1,0:T(8,128)(2,1)}, bf16[200,1024]{1,0:T(8,128)(2,1)}, u32[]{:S(2)}, u32[]{:S(2)}) collective-permute-start(bf16[200,1024]{1,0:T(8,128)(2,1)} %get-tuple-element.20), channel_id=1, source_target_pairs={{0,3},{1,2},{2,1},{3,0},{4,7},{5,6},{6,5},{7,4},{8,11},{9,10},{10,... | collective-permute-start | bytes 1228808 | tf_op jit(solution)/shard_map/ppermute | solution.py:39
  143.3 14.6 %collective-permute-start.20 = (bf16[128,1152]{1,0:T(8,128)(2,1)S(1)}, bf16[128,1152]{1,0:T(8,128)(2,1)S(1)}, u32[]{:S(2)}, u32[]{:S(2)}) collective-permute-start(bf16[128,1152]{1,0:T(8,128)(2,1)S(1)} %get-tuple-element.31), channel_id=1, source_target_pairs={{0,12},{1,13},{2,14},{3,15},{4,0},{5,1},{6,2},{7,3},{8,4},{9,5},{1... | collective-permute-start | bytes 884744 | tf_op jit(solution)/shard_map/ppermute | solution.py:34
  143.4 17.9 %collective-permute-start.22 = (bf16[128,1152]{1,0:T(8,128)(2,1)S(1)}, bf16[128,1152]{1,0:T(8,128)(2,1)S(1)}, u32[]{:S(2)}, u32[]{:S(2)}) collective-permute-start(bf16[128,1152]{1,0:T(8,128)(2,1)S(1)} %get-tuple-element.32), channel_id=1, source_target_pairs={{0,4},{1,5},{2,6},{3,7},{4,8},{5,9},{6,10},{7,11},{8,12},{9,13},{1... | collective-permute-start | bytes 884744 | tf_op jit(solution)/shard_map/ppermute | solution.py:34
  145.4 33.4 %collective-permute-start.21 = (bf16[128,1152]{1,0:T(8,128)(2,1)S(1)}, bf16[128,1152]{1,0:T(8,128)(2,1)S(1)}, u32[]{:S(2)}, u32[]{:S(2)}) collective-permute-start(bf16[128,1152]{1,0:T(8,128)(2,1)S(1)} %get-tuple-element.33), channel_id=1, source_target_pairs={{0,8},{1,9},{2,10},{3,11},{4,12},{5,13},{6,14},{7,15},{8,0},{9,1},... | collective-permute-start | bytes 884744 | tf_op jit(solution)/shard_map/ppermute | solution.py:34
  158.0 28.4 %collective-permute-start.25 = (bf16[128,1152]{1,0:T(8,128)(2,1)S(1)}, bf16[128,1152]{1,0:T(8,128)(2,1)S(1)}, u32[]{:S(2)}, u32[]{:S(2)}) collective-permute-start(bf16[128,1152]{1,0:T(8,128)(2,1)S(1)} %broadcast_add_fusion), channel_id=1, source_target_pairs={{0,12},{1,13},{2,14},{3,15},{4,0},{5,1},{6,2},{7,3},{8,4},{9,5},{1... | collective-permute-start | bytes 884744 | tf_op jit(solution)/shard_map/ppermute | solution.py:34
  161.3 22.3 %copy-start.18 = (bf16[128,1152]{1,0:T(8,128)(2,1)}, bf16[128,1152]{1,0:T(8,128)(2,1)S(1)}, u32[]{:S(2)}) copy-start(bf16[128,1152]{1,0:T(8,128)(2,1)S(1)} %collective-permute-done.22) | copy-start | bytes 884740
  161.3 34.5 %collective-permute-start.24 = (bf16[128,1152]{1,0:T(8,128)(2,1)S(1)}, bf16[128,1152]{1,0:T(8,128)(2,1)S(1)}, u32[]{:S(2)}, u32[]{:S(2)}) collective-permute-start(bf16[128,1152]{1,0:T(8,128)(2,1)S(1)} %broadcast_add_fusion), channel_id=1, source_target_pairs={{0,8},{1,9},{2,10},{3,11},{4,12},{5,13},{6,14},{7,15},{8,0},{9,1},... | collective-permute-start | bytes 884744 | tf_op jit(solution)/shard_map/ppermute | solution.py:34
  178.8 17.1 %collective-permute-start.23 = (bf16[128,1152]{1,0:T(8,128)(2,1)S(1)}, bf16[128,1152]{1,0:T(8,128)(2,1)S(1)}, u32[]{:S(2)}, u32[]{:S(2)}) collective-permute-start(bf16[128,1152]{1,0:T(8,128)(2,1)S(1)} %broadcast_add_fusion), channel_id=1, source_target_pairs={{0,4},{1,5},{2,6},{3,7},{4,8},{5,9},{6,10},{7,11},{8,12},{9,13},{1... | collective-permute-start | bytes 884744 | tf_op jit(solution)/shard_map/ppermute | solution.py:34
  185.9 33.5 %collective-permute-start.30 = (bf16[352,2048]{1,0:T(8,128)(2,1)}, bf16[352,2048]{1,0:T(8,128)(2,1)}, u32[]{:S(2)}, u32[]{:S(2)}) collective-permute-start(bf16[352,2048]{1,0:T(8,128)(2,1)} %fusion.74), channel_id=1, source_target_pairs={{0,16},{16,0},{1,17},{17,1},{2,18},{18,2},{3,19},{19,3},{4,20},{20... | collective-permute-start | bytes 4325384 | tf_op jit(solution)/shard_map/ppermute | solution.py:44
  207.0 15.1 %collective-permute-start.29 = (bf16[200,1024]{1,0:T(8,128)(2,1)S(1)}, bf16[200,1024]{1,0:T(8,128)(2,1)S(1)}, u32[]{:S(2)}, u32[]{:S(2)}) collective-permute-start(bf16[200,1024]{1,0:T(8,128)(2,1)S(1)} %get-tuple-element.24), channel_id=1, source_target_pairs={{0,3},{1,2},{2,1},{3,0},{4,7},{5,6},{6,5},{7,4},{8,11},{9,10},{10,... | collective-permute-start | bytes 1228808 | tf_op jit(solution)/shard_map/ppermute | solution.py:39
  207.1 20.6 %collective-permute-start.28 = (bf16[200,1024]{1,0:T(8,128)(2,1)S(1)}, bf16[200,1024]{1,0:T(8,128)(2,1)S(1)}, u32[]{:S(2)}, u32[]{:S(2)}) collective-permute-start(bf16[200,1024]{1,0:T(8,128)(2,1)S(1)} %get-tuple-element.25), channel_id=1, source_target_pairs={{0,2},{1,3},{2,0},{3,1},{4,6},{5,7},{6,4},{7,5},{8,10},{9,11},{10,... | collective-permute-start | bytes 1228808 | tf_op jit(solution)/shard_map/ppermute | solution.py:39
  208.6 19.0 %collective-permute-start.27 = (bf16[200,1024]{1,0:T(8,128)(2,1)S(1)}, bf16[200,1024]{1,0:T(8,128)(2,1)S(1)}, u32[]{:S(2)}, u32[]{:S(2)}) collective-permute-start(bf16[200,1024]{1,0:T(8,128)(2,1)S(1)} %get-tuple-element.26), channel_id=1, source_target_pairs={{0,1},{1,0},{2,3},{3,2},{4,5},{5,4},{6,7},{7,6},{8,9},{9,8},{10,11... | collective-permute-start | bytes 1228808 | tf_op jit(solution)/shard_map/ppermute | solution.py:39
  219.3 17.1 %collective-permute-start.42 = (bf16[200,1024]{1,0:T(8,128)(2,1)S(1)}, bf16[200,1024]{1,0:T(8,128)(2,1)S(1)}, u32[]{:S(2)}, u32[]{:S(2)}) collective-permute-start(bf16[200,1024]{1,0:T(8,128)(2,1)S(1)} %copy-done.15), channel_id=1, source_target_pairs={{0,2},{1,3},{2,0},{3,1},{4,6},{5,7},{6,4},{7,5},{8,10},{9,11},{10,... | collective-permute-start | bytes 1228808 | tf_op jit(solution)/shard_map/ppermute | solution.py:39
  222.1 15.4 %collective-permute-start.41 = (bf16[200,1024]{1,0:T(8,128)(2,1)S(1)}, bf16[200,1024]{1,0:T(8,128)(2,1)S(1)}, u32[]{:S(2)}, u32[]{:S(2)}) collective-permute-start(bf16[200,1024]{1,0:T(8,128)(2,1)S(1)} %copy-done.14), channel_id=1, source_target_pairs={{0,1},{1,0},{2,3},{3,2},{4,5},{5,4},{6,7},{7,6},{8,9},{9,8},{10,11... | collective-permute-start | bytes 1228808 | tf_op jit(solution)/shard_map/ppermute | solution.py:39
  231.5 30.0 %collective-permute-start.37 = (bf16[200,1024]{1,0:T(8,128)(2,1)S(1)}, bf16[200,1024]{1,0:T(8,128)(2,1)S(1)}, u32[]{:S(2)}, u32[]{:S(2)}) collective-permute-start(bf16[200,1024]{1,0:T(8,128)(2,1)S(1)} %get-tuple-element.16), channel_id=1, source_target_pairs={{0,3},{1,2},{2,1},{3,0},{4,7},{5,6},{6,5},{7,4},{8,11},{9,10},{10,... | collective-permute-start | bytes 1228808 | tf_op jit(solution)/shard_map/ppermute | solution.py:39
  232.7 28.8 %collective-permute-start.36 = (bf16[200,1024]{1,0:T(8,128)(2,1)S(1)}, bf16[200,1024]{1,0:T(8,128)(2,1)S(1)}, u32[]{:S(2)}, u32[]{:S(2)}) collective-permute-start(bf16[200,1024]{1,0:T(8,128)(2,1)S(1)} %get-tuple-element.17), channel_id=1, source_target_pairs={{0,2},{1,3},{2,0},{3,1},{4,6},{5,7},{6,4},{7,5},{8,10},{9,11},{10,... | collective-permute-start | bytes 1228808 | tf_op jit(solution)/shard_map/ppermute | solution.py:39
  233.2 28.2 %collective-permute-start.35 = (bf16[200,1024]{1,0:T(8,128)(2,1)S(1)}, bf16[200,1024]{1,0:T(8,128)(2,1)S(1)}, u32[]{:S(2)}, u32[]{:S(2)}) collective-permute-start(bf16[200,1024]{1,0:T(8,128)(2,1)S(1)} %get-tuple-element.18), channel_id=1, source_target_pairs={{0,1},{1,0},{2,3},{3,2},{4,5},{5,4},{6,7},{7,6},{8,9},{9,8},{10,11... | collective-permute-start | bytes 1228808 | tf_op jit(solution)/shard_map/ppermute | solution.py:39
  236.4 13.2 %collective-permute-start.31 = (bf16[128,1024]{1,0:T(8,128)(2,1)S(1)}, bf16[128,1024]{1,0:T(8,128)(2,1)S(1)}, u32[]{:S(2)}, u32[]{:S(2)}) collective-permute-start(bf16[128,1024]{1,0:T(8,128)(2,1)S(1)} %get-tuple-element.34), channel_id=1, source_target_pairs={{0,12},{1,13},{2,14},{3,15},{4,0},{5,1},{6,2},{7,3},{8,4},{9,5},{1... | collective-permute-start | bytes 786440 | tf_op jit(solution)/shard_map/ppermute | solution.py:34
  237.5 15.7 %collective-permute-start.33 = (bf16[128,1024]{1,0:T(8,128)(2,1)S(1)}, bf16[128,1024]{1,0:T(8,128)(2,1)S(1)}, u32[]{:S(2)}, u32[]{:S(2)}) collective-permute-start(bf16[128,1024]{1,0:T(8,128)(2,1)S(1)} %get-tuple-element.35), channel_id=1, source_target_pairs={{0,4},{1,5},{2,6},{3,7},{4,8},{5,9},{6,10},{7,11},{8,12},{9,13},{1... | collective-permute-start | bytes 786440 | tf_op jit(solution)/shard_map/ppermute | solution.py:34
  249.6 11.1 %collective-permute-start.32 = (bf16[128,1024]{1,0:T(8,128)(2,1)S(1)}, bf16[128,1024]{1,0:T(8,128)(2,1)S(1)}, u32[]{:S(2)}, u32[]{:S(2)}) collective-permute-start(bf16[128,1024]{1,0:T(8,128)(2,1)S(1)} %get-tuple-element.36), channel_id=1, source_target_pairs={{0,8},{1,9},{2,10},{3,11},{4,12},{5,13},{6,14},{7,15},{8,0},{9,1},... | collective-permute-start | bytes 786440 | tf_op jit(solution)/shard_map/ppermute | solution.py:34
  260.9 7.6 %collective-permute-start.34 = (bf16[128,1024]{1,0:T(8,128)(2,1)S(1)}, bf16[128,1024]{1,0:T(8,128)(2,1)S(1)}, u32[]{:S(2)}, u32[]{:S(2)}) collective-permute-start(bf16[128,1024]{1,0:T(8,128)(2,1)S(1)} %add_convert_fusion), channel_id=1, source_target_pairs={{0,16},{16,0},{1,17},{17,1},{2,18},{18,2},{3,19},{19,3},{4,20},{20... | collective-permute-start | bytes 786440 | tf_op jit(solution)/shard_map/ppermute | solution.py:44
  (43 other events, 268.0 us)
